TPU v7x, 32 devices: a whole 2x2x4 slice. The times are simulated.
32 devices in a mesh: group: 2 (over x), blk: 16 (over z, y, core).
Axes of the slice: x: 2, y: 2, z: 4, core: 2. Of those that a mesh axis runs over, the one named last changes fastest.
Arguments:
- coarse: float32 [3, 16384, 256], P(None, ('group', 'blk')), parts along dimension 1, may hold values from -6 to 6
- fine_old: float32 [192, 3, 32, 256], P(('group', 'blk')), parts along dimension 0, may hold values from -6 to 6
- refine_flags: int32 [1024], P('group'), parts along dimension 0, may hold values from 0 to 1, as said below
- new_slot: int32 [64], P('group'), parts along dimension 0, may hold values from 0 to 31, each once
- courant: float32 [512], P('group'), parts along dimension 0, may hold values from 0.05 to 0.9
Outputs:
- coarse_out: float32 [3, 16384, 256], P(None, ('group', 'blk')), parts along dimension 1
- fine_out: float32 [64, 3, 32, 256], P(('group', 'blk')), parts along dimension 0
There are 2 independent parts, one for each index of `group`. A program takes and returns all parts, laid end to end along the dimension named above; each array names one. Nothing has to cross between parts.
Inputs may be any that keep to these rules, and one draw needn't show every extreme that they name: `refine_flags`: no two flagged blocks are adjacent; the first and last block of each owner's aligned run of 32 blocks is never flagged; each run holds at most 6 flags, some run exactly 6; 32 flags in all. `new_slot`: each slot once.
All inputs are finite; a program needn't handle non-finite values.
Results may differ from a plain program's by a relative error of at most 0.00002.
Values sent between devices are 32-bit elements; how exact they have to be, the bound alone decides.
A program may use at most 64 MiB of HBM per device.

v0:
```python
import jax
import jax.numpy as jnp
from jax import lax
from jax.sharding import PartitionSpec as P

B_DEV = 32
CB = 16
FCAP = 6
F_DEV = 2


sound_number = 0.6


def padded_2(block, sides, width):
    for axis, dim in sides:
        count = lax.axis_size(axis)
        forward = [(i, i + 1) for i in range(count - 1)]
        forward.append((count - 1, 0))
        backward = [(target, source) for source, target in forward]
        low = lax.ppermute(
            lax.slice_in_dim(block, block.shape[dim] - width, None, axis=dim), axis, forward
        )
        high = lax.ppermute(lax.slice_in_dim(block, 0, width, axis=dim), axis, backward)
        block = jnp.concatenate([low, block, high], axis=dim)
    return block


def acoustic(pressure, velocity, rim_width):
    press_flux = sound_number * 0.5 * (pressure[:-1] + pressure[1:])
    velocity_new = velocity[1:-1] - (press_flux[1:] - press_flux[:-1])
    speed_flux = sound_number * 0.5 * (velocity_new[:-1] + velocity_new[1:])
    pressure_new = pressure[2:-2] - (speed_flux[1:] - speed_flux[:-1])
    cell_count = pressure.shape[0] - 2 * rim_width
    return (
        pressure_new,
        velocity_new[1:-1],
        speed_flux,
        press_flux[rim_width - 1 : rim_width + cell_count],
    )


def transport(warmth, courant):
    heat_flux = courant * 0.5 * (warmth[:-1] + warmth[1:]) - 0.5 * courant * courant * (
        warmth[1:] - warmth[:-1]
    )
    return (warmth[1:-1] - (heat_flux[1:] - heat_flux[:-1]), heat_flux)


def fine_steps(block, ghosts, courant):
    pressure, velocity, warmth = (block[0], block[1], block[2])
    nothing = jnp.zeros((block.shape[2],), jnp.float32)
    flux_left = [nothing, nothing, nothing]
    flux_right = [nothing, nothing, nothing]
    for fine_round in range(2):
        fraction = 0.5 * fine_round
        edge_values = ghosts[0:2] + fraction * (ghosts[2:4] - ghosts[0:2])
        left_edge, right_edge = (edge_values[0], edge_values[1])
        for substep in range(4):
            padded = jnp.concatenate([left_edge[0][None], pressure, right_edge[0][None]], 0)
            press_flux = sound_number * 0.5 * (padded[:-1] + padded[1:])
            velocity = velocity - (press_flux[1:] - press_flux[:-1])
            padded = jnp.concatenate([left_edge[1][None], velocity, right_edge[1][None]], 0)
            speed_flux = sound_number * 0.5 * (padded[:-1] + padded[1:])
            pressure = pressure - (speed_flux[1:] - speed_flux[:-1])
            flux_left = [flux_left[0] + speed_flux[0], flux_left[1] + press_flux[0], flux_left[2]]
            flux_right = [
                flux_right[0] + speed_flux[-1],
                flux_right[1] + press_flux[-1],
                flux_right[2],
            ]
        padded = jnp.concatenate([left_edge[2][None], warmth, right_edge[2][None]], 0)
        warmth, heat_flux = transport(padded, courant)
        flux_left = [flux_left[0], flux_left[1], flux_left[2] + heat_flux[0]]
        flux_right = [flux_right[0], flux_right[1], flux_right[2] + heat_flux[-1]]
    return (jnp.stack([pressure, velocity, warmth]), jnp.stack(flux_left), jnp.stack(flux_right))


def average_down(blocks):
    return 0.5 * (blocks[:, :, 0::2] + blocks[:, :, 1::2])


def apply_fine(field, face_sums, flag_row, avg_rows, reg_rows):
    block_count = flag_row.shape[0]
    columns = field.shape[2]
    blocks = field.reshape(3, block_count, CB, columns)
    refined = flag_row == 1
    left_fix = face_sums[:, :block_count] - 0.5 * reg_rows[:, 0].transpose(1, 0, 2)
    right_fix = face_sums[:, 1:] - 0.5 * reg_rows[:, 1].transpose(1, 0, 2)
    nothing = jnp.zeros_like(left_fix[:, :1])
    marked = refined[None, :, None]
    last_add = jnp.concatenate([jnp.where(marked, left_fix, 0.0)[:, 1:], nothing], 1)
    first_add = jnp.concatenate([nothing, jnp.where(marked, -right_fix, 0.0)[:, :-1]], 1)
    blocks = jnp.where(refined[None, :, None, None], avg_rows.transpose(1, 0, 2, 3), blocks)
    blocks = blocks.at[:, :, CB - 1].add(last_add).at[:, :, 0].add(first_add)
    return blocks.reshape(3, block_count * CB, columns)


def coarse_step(coarse, courant):
    press_sum = jnp.zeros((coarse.shape[1] + 1, coarse.shape[2]), jnp.float32)
    speed_sum = press_sum
    padded = padded_2(coarse, (("blk", 1),), 2)
    pressure, velocity = (padded[0], padded[1])
    warmth = padded[2][1:-1]
    for substep in range(4):
        if substep > 0:
            pair_rim = padded_2(jnp.stack([pressure, velocity]), (("blk", 1),), 2)
            pressure, velocity = (pair_rim[0], pair_rim[1])
        pressure, velocity, speed_flux, press_flux = acoustic(pressure, velocity, 2)
        speed_sum = speed_sum + speed_flux
        press_sum = press_sum + press_flux
    warmth, heat_flux = transport(warmth, courant)
    face_sums = jnp.stack([speed_sum[::CB], press_sum[::CB], heat_flux[::CB]])
    return (jnp.stack([pressure, velocity, warmth]), face_sums)


def per_device(coarse, fine_old, refine_flags, new_slot, courant):
    rank_here = lax.axis_index("blk")
    fine_count = new_slot.shape[0]
    flag_total = jnp.cumsum(refine_flags)
    before = flag_total - refine_flags
    my_flags = lax.dynamic_slice_in_dim(refine_flags, rank_here * B_DEV, B_DEV)
    my_ids = lax.dynamic_slice_in_dim(flag_total, rank_here * B_DEV, B_DEV) - 1
    first_id = lax.dynamic_slice_in_dim(before, rank_here * B_DEV, 1)[0]
    my_rank = jnp.cumsum(my_flags) - 1
    slot_ids = jnp.arange(FCAP, dtype=jnp.int32)
    block_ids = jnp.arange(B_DEV, dtype=jnp.int32)
    slot_hit = (my_flags[None, :] == 1) & (my_rank[None, :] == slot_ids[:, None])
    slot_live = jnp.any(slot_hit, axis=1)
    slot_block = jnp.where(
        slot_live, jnp.sum(jnp.where(slot_hit, block_ids[None, :], 0), axis=1), 1
    )
    slot_fine = jnp.clip(first_id + slot_ids, 0, fine_count - 1)
    slot_dest = jnp.where(slot_live, new_slot[slot_fine], -1)
    row_ids = jnp.arange(fine_count, dtype=jnp.int32)
    send_match = slot_dest[None, :] == row_ids[:, None]
    send_slot = jnp.sum(jnp.where(send_match, slot_ids[None, :], 0), axis=1)
    send_live = jnp.any(send_match, axis=1)
    targets = rank_here * F_DEV + jnp.arange(F_DEV, dtype=jnp.int32)
    target_fine = jnp.sum(
        jnp.where(new_slot[None, :] == targets[:, None], row_ids[None, :], 0), axis=1
    )
    parents = jnp.nonzero(refine_flags, size=fine_count)[0].astype(jnp.int32)
    sources = parents[target_fine] // B_DEV
    pick_rows = sources * F_DEV + jnp.arange(F_DEV, dtype=jnp.int32)
    block_rows = new_slot[jnp.clip(my_ids, 0, fine_count - 1)]

    def route(packed):
        shaped = send_live.reshape((fine_count,) + (1,) * (packed.ndim - 1))
        return jnp.where(shaped, packed[send_slot], 0.0)

    arrived = lax.all_to_all(route(fine_old), "blk", split_axis=0, concat_axis=0, tiled=True)
    my_blocks = arrived[pick_rows]
    advanced, face_sums = coarse_step(coarse, courant)
    edge_index = jnp.stack([slot_block * CB - 1, (slot_block + 1) * CB], 1)
    ghost_in = lax.all_to_all(
        route(
            jnp.concatenate([coarse[:, edge_index], advanced[:, edge_index]], 2).transpose(
                1, 2, 0, 3
            )
        ),
        "blk",
        split_axis=0,
        concat_axis=0,
        tiled=True,
    )[pick_rows]
    fine_new, left_regs, right_regs = jax.vmap(fine_steps, (0, 0, None))(
        my_blocks, ghost_in, courant
    )
    averaged = average_down(fine_new)
    registers = jnp.stack([left_regs, right_regs], 1)
    row_slot = row_ids % F_DEV
    keep_rows = sources[row_slot] == row_ids // F_DEV
    avg_send = jnp.where(keep_rows[:, None, None, None], averaged[row_slot], 0.0)
    reg_send = jnp.where(keep_rows[:, None, None, None], registers[row_slot], 0.0)
    avg_back, reg_back = (
        lax.all_to_all(avg_send, "blk", split_axis=0, concat_axis=0, tiled=True),
        lax.all_to_all(reg_send, "blk", split_axis=0, concat_axis=0, tiled=True),
    )
    coarse_out = apply_fine(
        advanced, face_sums, my_flags, avg_back[block_rows], reg_back[block_rows]
    )
    return (coarse_out, fine_new)


def solution(mesh):
    placed = (
        P(None, ("group", "blk"), None),
        P(("group", "blk"), None, None, None),
        P("group"),
        P("group"),
        P("group"),
    )
    return jax.shard_map(
        per_device,
        mesh=mesh,
        in_specs=placed,
        out_specs=(P(None, ("group", "blk"), None), P(("group", "blk"), None, None, None)),
        check_vma=False,
    )
```

profile of v0, /device:TPU:15, one launch (start us, length us, event | category | flops | bytes accessed | tf_op | source)
XLA Modules:
  0.0 218.4 jit_solution(18102810670525655085)
XLA Ops:
  1.5 1.8 collective-permute-start
  6.5 1.4 convert_reduce_fusion
  9.1 1.3 gather_fusion.1
  11.5 1.5 pad_maximum_fusion.1
  13.4 1.3 copy-done.2
  16.4 2.6 %collective-permute-start.2 = (f32[2,2,256]{2,1,0:T(2,128)S(1)}, f32[2,2,256]{2,1,0:T(2,128)S(1)}, u32[]{:S(2)}, u32[]{:S(2)}) collective-permute-start(f32[2,2,256]{2,1,0:T(2,128)S(1)} %get-tuple-element.46), channel_id=1, source_target_pairs={{0,1},{1,2},{2,3},{3,4},{4,5},{5,6},{6,7},{7,8},{8,9},{9,10},{10,1... | collective-permute-start | bytes 12296 | tf_op jit(solution)/shard_map/ppermute | solution.py:21
  19.8 3.2 %collective-permute-done.3 = f32[2,2,256]{2,1,0:T(2,128)S(1)} collective-permute-done((f32[2,2,256]{2,1,0:T(2,128)S(1)}, f32[2,2,256]{2,1,0:T(2,128)S(1)}, u32[]{:S(2)}, u32[]{:S(2)}) %collective-permute-start.3) | collective-permute-done | bytes 4128 | tf_op jit(solution)/shard_map/ppermute | solution.py:24
  22.9 1.3 pad_maximum_fusion.2
  27.5 2.8 %collective-permute-done.5 = f32[2,2,256]{2,1,0:T(2,128)S(1)} collective-permute-done((f32[2,2,256]{2,1,0:T(2,128)S(1)}, f32[2,2,256]{2,1,0:T(2,128)S(1)}, u32[]{:S(2)}, u32[]{:S(2)}) %collective-permute-start.5) | collective-permute-done | bytes 4128 | tf_op jit(solution)/shard_map/ppermute | solution.py:24
  32.7 2.8 %collective-permute-done.7 = f32[2,2,256]{2,1,0:T(2,128)S(1)} collective-permute-done((f32[2,2,256]{2,1,0:T(2,128)S(1)}, f32[2,2,256]{2,1,0:T(2,128)S(1)}, u32[]{:S(2)}, u32[]{:S(2)}) %collective-permute-start.7) | collective-permute-done | bytes 4128 | tf_op jit(solution)/shard_map/ppermute | solution.py:24
  39.1 2.7 %pad_maximum_fusion = f32[3,512,256]{2,0,1:T(4,128)} fusion(f32[1,512,256]{2,0,1:T(1,128)S(1)} %stack.103, f32[1,512,256]{2,0,1:T(1,128)S(1)} %copy.79, f32[1,512,256]{2,0,1:T(1,128)S(1)} %copy.78), kind=kLoop, calls=%fused_computation.14 | loop fusion | flops 786432 | bytes 3145728 | tf_op jit(solution)/shard_map/stack | solution.py:114
  41.8 2.2 gather_fusion.5
  45.7 11.8 %all-to-all-start.1 = ((f32[32,4,3,256]{3,1,2,0:T(4,128)}), f32[32,4,3,256]{3,1,2,0:T(4,128)S(1)}, u32[]{:S(2)}, u32[]{:S(2)}) async-start(f32[32,4,3,256]{3,1,2,0:T(4,128)} %broadcast_select_fusion.2), calls=%async_computation.1 | async-start | bytes 786432 | tf_op jit(solution)/shard_map/all_to_all | solution.py:156
  57.6 2.4 %gather_fusion.2 = f32[32,3,32,256]{3,2,1,0:T(8,128)} fusion(f32[6,3,32,256]{3,2,1,0:T(8,128)S(1)} %copy-done, s32[1024]{0:T(1024)S(1)} %pad_clamp_fusion.5), kind=kCustom, calls=%fused_computation.2 | custom fusion | bytes 6291584 | tf_op jit(solution)/shard_map/gather | solution.py:150
  60.0 4.2 %broadcast_select_fusion = f32[32,3,32,256]{3,2,1,0:T(8,128)} fusion(f32[32,3,32,256]{3,2,1,0:T(8,128)} %gather_fusion.2, pred[32]{0:T(512)(128)(4,1)S(1)} %fusion.76), kind=kLoop, calls=%fused_computation.17 | loop fusion | flops 786432 | bytes 6291488 | tf_op jit(solution)/shard_map/jit(_where)/select_n | solution.py:150
  64.1 4.2 %all-to-all-done.1 = f32[32,4,3,256]{3,1,2,0:T(4,128)S(1)} async-done(((f32[32,4,3,256]{3,1,2,0:T(4,128)}), f32[32,4,3,256]{3,1,2,0:T(4,128)S(1)}, u32[]{:S(2)}, u32[]{:S(2)}) %all-to-all-start.1) | async-done | bytes 393248 | tf_op jit(solution)/shard_map/all_to_all | solution.py:156
  68.3 5.8 %all-to-all-start = ((f32[32,3,32,256]{3,2,1,0:T(8,128)}), f32[32,3,32,256]{3,2,1,0:T(8,128)}, u32[]{:S(2)}, u32[]{:S(2)}) async-start(f32[32,3,32,256]{3,2,1,0:T(8,128)} %broadcast_select_fusion), calls=%async_computation | async-start | bytes 6291456 | tf_op jit(solution)/shard_map/all_to_all | solution.py:152
  74.7 4.1 %scatter_custom_fusion = s32[32]{0:T(128)S(1)} fusion(s32[512]{0:T(512)S(1)} %bitcast.158, s32[512]{0:T(512)S(1)} %broadcast.577, s32[]{:T(128)} %constant.157.clone.1), kind=kCustom, calls=%fused_computation.317 | custom fusion | flops 512 | bytes 132 | tf_op jit(solution)/shard_map/scatter-add | solution.py:143
  81.3 1.3 fusion.86
  83.3 60.8 %all-to-all-done = f32[32,3,32,256]{3,2,1,0:T(8,128)} async-done(((f32[32,3,32,256]{3,2,1,0:T(8,128)}), f32[32,3,32,256]{3,2,1,0:T(8,128)}, u32[]{:S(2)}, u32[]{:S(2)}) %all-to-all-start) | async-done | bytes 3145760 | tf_op jit(solution)/shard_map/all_to_all | solution.py:152
  144.1 2.4 %gather_fusion.3 = f32[2,3,32,256]{3,2,1,0:T(8,128)S(1)} fusion(f32[32,3,32,256]{3,2,1,0:T(8,128)} %all-to-all-done, s32[1024]{0:T(1024)S(1)} %pad_clamp_fusion.4), kind=kCustom, calls=%fused_computation.3 | custom fusion | bytes 393224 | tf_op jit(solution)/shard_map/gather | solution.py:153
  149.5 5.1 %all-to-all-start.3 = ((f32[32,2,3,256]{3,1,2,0:T(2,128)}), f32[32,2,3,256]{3,1,2,0:T(2,128)S(1)}, u32[]{:S(2)}, u32[]{:S(2)}) async-start(f32[32,2,3,256]{3,1,2,0:T(2,128)} %copy.84), calls=%async_computation.3 | async-start | bytes 393216 | tf_op jit(solution)/shard_map/all_to_all | solution.py:178
  154.6 1.8 gather_fusion.8
  156.3 2.7 %broadcast_select_fusion.1 = f32[32,3,16,256]{3,2,1,0:T(8,128)} fusion(f32[32,3,16,256]{3,2,1,0:T(8,128)} %gather_fusion.8, pred[32]{0:T(512)(128)(4,1)S(1)} %fusion.86), kind=kLoop, calls=%fused_computation.21 | loop fusion | flops 393216 | bytes 3145760 | tf_op jit(solution)/shard_map/jit(_where)/select_n | solution.py:174
  159.1 2.0 all-to-all-done.3
  161.1 6.7 %all-to-all-start.2 = ((f32[32,3,16,256]{3,2,1,0:T(8,128)}), f32[32,3,16,256]{3,2,1,0:T(8,128)}, u32[]{:S(2)}, u32[]{:S(2)}) async-start(f32[32,3,16,256]{3,2,1,0:T(8,128)} %broadcast_select_fusion.1), calls=%async_computation.2 | async-start | bytes 3145728 | tf_op jit(solution)/shard_map/all_to_all | solution.py:177
  174.8 29.3 %all-to-all-done.2 = f32[32,3,16,256]{3,2,1,0:T(8,128)} async-done(((f32[32,3,16,256]{3,2,1,0:T(8,128)}), f32[32,3,16,256]{3,2,1,0:T(8,128)}, u32[]{:S(2)}, u32[]{:S(2)}) %all-to-all-start.2) | async-done | bytes 1572896 | tf_op jit(solution)/shard_map/all_to_all | solution.py:177
  204.1 3.2 %gather_fusion.10 = f32[32,3,16,256]{3,2,1,0:T(8,128)} fusion(f32[32,3,16,256]{3,2,1,0:T(8,128)} %all-to-all-done.2, s32[1024]{0:T(1024)S(1)} %pad_clamp_fusion), kind=kCustom, calls=%fused_computation.10 | custom fusion | bytes 3145856 | tf_op jit(solution)/shard_map/gather | solution.py:181
  207.3 1.8 maximum_select_fusion
  209.3 3.8 %scatter-add.18 = f32[3,32,16,256]{3,2,0,1:T(8,128)S(1)} dynamic-update-slice(f32[3,32,16,256]{3,2,0,1:T(8,128)S(1)} %maximum_select_fusion, f32[3,32,1,256]{3,2,0,1:T(1,128)S(1)} %slice_add_fusion.12, s32[]{:T(128)} %constant.157.clone.1, s32[]{:T(128)} %constant.157.clone.1, s32[]{:T(128)} %constant.171.clone.1, s32[]{:T(128)} %constant.157.clone.1) | dynamic-update-slice | bytes 196612 | tf_op jit(solution)/shard_map/scatter-add | solution.py:95
  213.3 3.8 %scatter-add.19 = f32[3,32,16,256]{3,2,0,1:T(8,128)S(1)} dynamic-update-slice(f32[3,32,16,256]{3,2,0,1:T(8,128)S(1)} %scatter-add.18, f32[3,32,1,256]{3,2,0,1:T(1,128)S(1)} %slice_add_fusion.11, s32[]{:T(128)} %constant.157.clone.1, s32[]{:T(128)} %constant.157.clone.1, s32[]{:T(128)} %constant.157.clone.1, s32[]{:T(128)} %constant.157.clone.1) | dynamic-update-slice | bytes 196612 | tf_op jit(solution)/shard_map/scatter-add | solution.py:95
  217.1 1.3 copy.89
  (202 shorter events, 33.3 us)
Async XLA Ops:
  0.6 56.9 %copy-start = (f32[6,3,32,256]{3,2,1,0:T(8,128)S(1)}, f32[6,3,32,256]{3,2,1,0:T(8,128)}, u32[]{:S(2)}) copy-start(f32[6,3,32,256]{3,2,1,0:T(8,128)} %param.10) | copy-start | bytes 1769476
  1.5 10.0 %collective-permute-start = (f32[3,2,256]{2,1,0:T(2,128)S(1)}, f32[3,2,256]{2,1,0:T(2,128)S(1)}, u32[]{:S(2)}, u32[]{:S(2)}) collective-permute-start(f32[3,2,256]{2,1,0:T(2,128)S(1)} %get-tuple-element.41), channel_id=1, source_target_pairs={{0,1},{1,2},{2,3},{3,4},{4,5},{5,6},{6,7},{7,8},{8,9},{9,10},{10,1... | collective-permute-start | bytes 18440 | tf_op jit(solution)/shard_map/ppermute | solution.py:21
  3.3 8.3 %collective-permute-start.1 = (f32[3,2,256]{2,1,0:T(2,128)S(1)}, f32[3,2,256]{2,1,0:T(2,128)S(1)}, u32[]{:S(2)}, u32[]{:S(2)}) collective-permute-start(f32[3,2,256]{2,1,0:T(2,128)S(1)} %get-tuple-element.40), channel_id=1, source_target_pairs={{1,0},{2,1},{3,2},{4,3},{5,4},{6,5},{7,6},{8,7},{9,8},{10,9},{11,1... | collective-permute-start | bytes 18440 | tf_op jit(solution)/shard_map/ppermute | solution.py:24
  13.3 1.4 copy-start.2
  14.7 1.7 copy-start.13
  16.4 3.4 %collective-permute-start.2 = (f32[2,2,256]{2,1,0:T(2,128)S(1)}, f32[2,2,256]{2,1,0:T(2,128)S(1)}, u32[]{:S(2)}, u32[]{:S(2)}) collective-permute-start(f32[2,2,256]{2,1,0:T(2,128)S(1)} %get-tuple-element.46), channel_id=1, source_target_pairs={{0,1},{1,2},{2,3},{3,4},{4,5},{5,6},{6,7},{7,8},{8,9},{9,10},{10,1... | collective-permute-start | bytes 12296 | tf_op jit(solution)/shard_map/ppermute | solution.py:21
  19.0 3.9 %collective-permute-start.3 = (f32[2,2,256]{2,1,0:T(2,128)S(1)}, f32[2,2,256]{2,1,0:T(2,128)S(1)}, u32[]{:S(2)}, u32[]{:S(2)}) collective-permute-start(f32[2,2,256]{2,1,0:T(2,128)S(1)} %get-tuple-element.47), channel_id=1, source_target_pairs={{1,0},{2,1},{3,2},{4,3},{5,4},{6,5},{7,6},{8,7},{9,8},{10,9},{11,1... | collective-permute-start | bytes 12296 | tf_op jit(solution)/shard_map/ppermute | solution.py:24
  24.3 0.8 copy-start.3
  26.3 1.2 collective-permute-start.4
  26.4 4.0 %collective-permute-start.5 = (f32[2,2,256]{2,1,0:T(2,128)S(1)}, f32[2,2,256]{2,1,0:T(2,128)S(1)}, u32[]{:S(2)}, u32[]{:S(2)}) collective-permute-start(f32[2,2,256]{2,1,0:T(2,128)S(1)} %get-tuple-element.45), channel_id=1, source_target_pairs={{1,0},{2,1},{3,2},{4,3},{5,4},{6,5},{7,6},{8,7},{9,8},{10,9},{11,1... | collective-permute-start | bytes 12296 | tf_op jit(solution)/shard_map/ppermute | solution.py:24
  27.0 5.0 %copy-start.7 = (f32[513,256]{1,0:T(8,128)}, f32[513,256]{1,0:T(8,128)S(1)}, u32[]{:S(2)}) copy-start(f32[513,256]{1,0:T(8,128)S(1)} %fusion.13) | copy-start | bytes 1575940
  30.5 0.8 copy-start.5
  31.4 1.2 collective-permute-start.6
  31.5 4.0 %collective-permute-start.7 = (f32[2,2,256]{2,1,0:T(2,128)S(1)}, f32[2,2,256]{2,1,0:T(2,128)S(1)}, u32[]{:S(2)}, u32[]{:S(2)}) collective-permute-start(f32[2,2,256]{2,1,0:T(2,128)S(1)} %get-tuple-element.43), channel_id=1, source_target_pairs={{1,0},{2,1},{3,2},{4,3},{5,4},{6,5},{7,6},{8,7},{9,8},{10,9},{11,1... | collective-permute-start | bytes 12296 | tf_op jit(solution)/shard_map/ppermute | solution.py:24
  32.1 3.5 %copy-start.10 = (f32[512,256]{1,0:T(8,128)}, f32[512,256]{1,0:T(8,128)S(1)}, u32[]{:S(2)}) copy-start(f32[512,256]{1,0:T(8,128)S(1)} %fusion.14) | copy-start | bytes 1572868
  37.0 1.5 copy-start.8
  37.1 0.9 copy-start.12
  45.7 22.6 %all-to-all-start.1 = ((f32[32,4,3,256]{3,1,2,0:T(4,128)}), f32[32,4,3,256]{3,1,2,0:T(4,128)S(1)}, u32[]{:S(2)}, u32[]{:S(2)}) async-start(f32[32,4,3,256]{3,1,2,0:T(4,128)} %broadcast_select_fusion.2), calls=%async_computation.1 | async-start | bytes 786432 | tf_op jit(solution)/shard_map/all_to_all | solution.py:156
  64.1 14.9 %copy-start.1 = (s32[32]{0:T(128)S(1)}, s32[32]{0:T(128)}, u32[]{:S(2)}) copy-start(s32[32]{0:T(128)} %param.12) | copy-start | bytes 388
  68.3 75.8 %all-to-all-start = ((f32[32,3,32,256]{3,2,1,0:T(8,128)}), f32[32,3,32,256]{3,2,1,0:T(8,128)}, u32[]{:S(2)}, u32[]{:S(2)}) async-start(f32[32,3,32,256]{3,2,1,0:T(8,128)} %broadcast_select_fusion), calls=%async_computation | async-start | bytes 6291456 | tf_op jit(solution)/shard_map/all_to_all | solution.py:152
  149.5 11.6 %all-to-all-start.3 = ((f32[32,2,3,256]{3,1,2,0:T(2,128)}), f32[32,2,3,256]{3,1,2,0:T(2,128)S(1)}, u32[]{:S(2)}, u32[]{:S(2)}) async-start(f32[32,2,3,256]{3,1,2,0:T(2,128)} %copy.84), calls=%async_computation.3 | async-start | bytes 393216 | tf_op jit(solution)/shard_map/all_to_all | solution.py:178
  159.1 10.6 %copy-start.4 = (f32[1,515,256]{2,1,0:T(8,128)S(1)}, f32[1,515,256]{2,1,0:T(8,128)}, u32[]{:S(2)}) copy-start(f32[1,515,256]{2,1,0:T(8,128)} %copy-done.3) | copy-start | bytes 1582084
  159.1 10.6 %copy-start.6 = (f32[1,515,256]{2,1,0:T(8,128)S(1)}, f32[1,515,256]{2,1,0:T(8,128)}, u32[]{:S(2)}) copy-start(f32[1,515,256]{2,1,0:T(8,128)} %copy-done.5) | copy-start | bytes 1582084
  161.1 43.0 %all-to-all-start.2 = ((f32[32,3,16,256]{3,2,1,0:T(8,128)}), f32[32,3,16,256]{3,2,1,0:T(8,128)}, u32[]{:S(2)}, u32[]{:S(2)}) async-start(f32[32,3,16,256]{3,2,1,0:T(8,128)} %broadcast_select_fusion.1), calls=%async_computation.2 | async-start | bytes 3145728 | tf_op jit(solution)/shard_map/all_to_all | solution.py:177
  174.7 32.6 %copy-start.9 = (f32[1,512,256]{2,1,0:T(8,128)S(1)}, f32[1,512,256]{2,1,0:T(8,128)}, u32[]{:S(2)}) copy-start(f32[1,512,256]{2,1,0:T(8,128)} %copy-done.8) | copy-start | bytes 1572868
  174.8 32.6 %copy-start.11 = (f32[512,256]{1,0:T(8,128)S(1)}, f32[512,256]{1,0:T(8,128)}, u32[]{:S(2)}) copy-start(f32[512,256]{1,0:T(8,128)} %copy-done.10) | copy-start | bytes 1572868
where the time goes:
time: 220 us; the launch traced here: 218 us
  waiting for transfers between devices  106 us (48%)
  local copies, waits for them, and re-layouts  40.8 us (19%)
  other arithmetic  35.1 us (16%)
  starting transfers between devices  35 us (16%)
    all_to_all x1, waiting for transfers between devices, per_device(): lax.all_to_all(route(fine_old), 'blk', split_axis=0, concat_axis=0, tiled...  60.8 us
    all_to_all x1, waiting for transfers between devices, per_device(): lax.all_to_all(avg_send, 'blk', split_axis=0, concat_axis=0, tiled=True)  29.3 us
    all_to_all x1, starting transfers between devices, per_device(): lax.all_to_all(route(jnp.concatenate([coarse[:, edge_index], advanced[:,...  11.8 us
    scatter-add x3, local copies, waits for them, and re-layouts, apply_fine(): blocks = blocks.at[:, :, CB - 1].add(last_add).at[:, :, 0].add(first_add)  8.98 us
    ppermute x4, waiting for transfers between devices, padded_2(): lax.ppermute(lax.slice_in_dim(block, 0, width, axis=dim), axis, backward)  8.84 us
    all_to_all x1, starting transfers between devices, per_device(): lax.all_to_all(avg_send, 'blk', split_axis=0, concat_axis=0, tiled=True)  6.71 us
    all_to_all x1, starting transfers between devices, per_device(): lax.all_to_all(route(fine_old), 'blk', split_axis=0, concat_axis=0, tiled...  5.78 us
    all_to_all x1, starting transfers between devices, per_device(): lax.all_to_all(reg_send, 'blk', split_axis=0, concat_axis=0, tiled=True)  5.07 us
  transfers between devices with their start and end apart: 12, of which 10 were waited for; matrix products, arithmetic and copies ran while one was open for 17% of the time, Pallas kernels for 0%

commit v1 on v0

v1 whole, which is shorter than its diff:
```python
import jax
import jax.numpy as jnp
from jax import lax
from jax.sharding import PartitionSpec as P

B_DEV = 32
CB = 16
FCAP = 6
F_DEV = 2


sound_number = 0.6


def transport(warmth, courant):
    heat_flux = courant * 0.5 * (warmth[:-1] + warmth[1:]) - 0.5 * courant * courant * (
        warmth[1:] - warmth[:-1]
    )
    return (warmth[1:-1] - (heat_flux[1:] - heat_flux[:-1]), heat_flux)


def fine_steps(block, ghosts, courant):
    pressure, velocity, warmth = (block[0], block[1], block[2])
    nothing = jnp.zeros((block.shape[2],), jnp.float32)
    flux_left = [nothing, nothing, nothing]
    flux_right = [nothing, nothing, nothing]
    for fine_round in range(2):
        fraction = 0.5 * fine_round
        edge_values = ghosts[0:2] + fraction * (ghosts[2:4] - ghosts[0:2])
        left_edge, right_edge = (edge_values[0], edge_values[1])
        for substep in range(4):
            padded = jnp.concatenate([left_edge[0][None], pressure, right_edge[0][None]], 0)
            press_flux = sound_number * 0.5 * (padded[:-1] + padded[1:])
            velocity = velocity - (press_flux[1:] - press_flux[:-1])
            padded = jnp.concatenate([left_edge[1][None], velocity, right_edge[1][None]], 0)
            speed_flux = sound_number * 0.5 * (padded[:-1] + padded[1:])
            pressure = pressure - (speed_flux[1:] - speed_flux[:-1])
            flux_left = [flux_left[0] + speed_flux[0], flux_left[1] + press_flux[0], flux_left[2]]
            flux_right = [
                flux_right[0] + speed_flux[-1],
                flux_right[1] + press_flux[-1],
                flux_right[2],
            ]
        padded = jnp.concatenate([left_edge[2][None], warmth, right_edge[2][None]], 0)
        warmth, heat_flux = transport(padded, courant)
        flux_left = [flux_left[0], flux_left[1], flux_left[2] + heat_flux[0]]
        flux_right = [flux_right[0], flux_right[1], flux_right[2] + heat_flux[-1]]
    return (jnp.stack([pressure, velocity, warmth]), jnp.stack(flux_left), jnp.stack(flux_right))


def average_down(blocks):
    return 0.5 * (blocks[:, :, 0::2] + blocks[:, :, 1::2])


def apply_fine(field, face_sums, flag_row, avg_rows, reg_rows):
    block_count = flag_row.shape[0]
    columns = field.shape[2]
    blocks = field.reshape(3, block_count, CB, columns)
    refined = flag_row == 1
    left_fix = face_sums[:, :block_count] - 0.5 * reg_rows[:, 0].transpose(1, 0, 2)
    right_fix = face_sums[:, 1:] - 0.5 * reg_rows[:, 1].transpose(1, 0, 2)
    nothing = jnp.zeros_like(left_fix[:, :1])
    marked = refined[None, :, None]
    last_add = jnp.concatenate([jnp.where(marked, left_fix, 0.0)[:, 1:], nothing], 1)
    first_add = jnp.concatenate([nothing, jnp.where(marked, -right_fix, 0.0)[:, :-1]], 1)
    blocks = jnp.where(refined[None, :, None, None], avg_rows.transpose(1, 0, 2, 3), blocks)
    blocks = blocks.at[:, :, CB - 1].add(last_add).at[:, :, 0].add(first_add)
    return blocks.reshape(3, block_count * CB, columns)


def halo_rows(block, width):
    count = lax.axis_size("blk")
    forward = [(i, (i + 1) % count) for i in range(count)]
    backward = [(target, source) for source, target in forward]
    low = lax.ppermute(block[:, -width:], "blk", forward)
    high = lax.ppermute(block[:, :width], "blk", backward)
    return jnp.concatenate([low, block, high], axis=1)


def coarse_step(coarse, courant):
    rows = coarse.shape[1]
    padded = halo_rows(coarse, 8)
    pressure, velocity = padded[0], padded[1]
    speed_sum = press_sum = 0.0
    for substep in range(4):
        press_flux = sound_number * 0.5 * (pressure[:-1] + pressure[1:])
        velocity = velocity[1:-1] - (press_flux[1:] - press_flux[:-1])
        speed_flux = sound_number * 0.5 * (velocity[:-1] + velocity[1:])
        pressure = pressure[2:-2] - (speed_flux[1:] - speed_flux[:-1])
        velocity = velocity[1:-1]
        rim = 6 - 2 * substep
        speed_sum = speed_sum + speed_flux[rim : rim + rows + 1]
        press_sum = press_sum + press_flux[rim + 1 : rim + 2 + rows]
    warmth, heat_flux = transport(padded[2][7:-7], courant)
    face_sums = jnp.stack([speed_sum[::CB], press_sum[::CB], heat_flux[::CB]])
    return (jnp.stack([pressure, velocity, warmth]), face_sums)


def per_device(coarse, fine_old, refine_flags, new_slot, courant):
    rank_here = lax.axis_index("blk")
    fine_count = new_slot.shape[0]
    block_all = jnp.arange(refine_flags.shape[0], dtype=jnp.int32)
    first_id = jnp.sum(jnp.where(block_all < rank_here * B_DEV, refine_flags, 0))
    my_flags = lax.dynamic_slice_in_dim(refine_flags, rank_here * B_DEV, B_DEV)
    block_ids = jnp.arange(B_DEV, dtype=jnp.int32)
    my_rank = jnp.sum(jnp.where(block_ids[None, :] < block_ids[:, None], my_flags[None, :], 0), axis=1)
    slot_ids = jnp.arange(FCAP, dtype=jnp.int32)
    slot_hit = (my_flags[None, :] == 1) & (my_rank[None, :] == slot_ids[:, None])
    slot_live = jnp.any(slot_hit, axis=1)
    slot_block = jnp.where(
        slot_live, jnp.sum(jnp.where(slot_hit, block_ids[None, :], 0), axis=1), 1
    )
    slot_fine = jnp.clip(first_id + slot_ids, 0, fine_count - 1)
    slot_dest = jnp.where(slot_live, new_slot[slot_fine], -1)
    row_ids = jnp.arange(fine_count, dtype=jnp.int32)
    send_match = slot_dest[None, :] == row_ids[:, None]
    send_slot = jnp.sum(jnp.where(send_match, slot_ids[None, :], 0), axis=1)
    send_live = jnp.any(send_match, axis=1)
    advanced, face_sums = coarse_step(coarse, courant)
    edge_index = jnp.stack([slot_block * CB - 1, (slot_block + 1) * CB], 1)
    ghosts = jnp.concatenate([coarse[:, edge_index], advanced[:, edge_index]], 2).transpose(
        1, 2, 0, 3
    )
    fine_new, left_regs, right_regs = jax.vmap(fine_steps, (0, 0, None))(
        fine_old, ghosts, courant
    )
    packed = jnp.where(send_live[:, None, None, None], fine_new[send_slot], 0.0)
    fine_out = lax.psum_scatter(packed, "blk", scatter_dimension=0, tiled=True)
    averaged = average_down(fine_new)
    registers = jnp.stack([left_regs, right_regs], 1)
    block_rows = jnp.clip(my_rank, 0, FCAP - 1)
    coarse_out = apply_fine(
        advanced, face_sums, my_flags, averaged[block_rows], registers[block_rows]
    )
    return (coarse_out, fine_out)


def solution(mesh):
    placed = (
        P(None, ("group", "blk"), None),
        P(("group", "blk"), None, None, None),
        P("group"),
        P("group"),
        P("group"),
    )
    return jax.shard_map(
        per_device,
        mesh=mesh,
        in_specs=placed,
        out_specs=(P(None, ("group", "blk"), None), P(("group", "blk"), None, None, None)),
        check_vma=False,
    )
```

time: 220 us -> 122 us (0.55)
  the two profiles are of different devices: /device:TPU:15 before, /device:TPU:0 now
where the time goes in v1:
time: 122 us; the launch traced here: 121 us
  waiting for transfers between devices  46.1 us (38%)
  local copies, waits for them, and re-layouts  32.7 us (27%)
  other arithmetic  21.6 us (18%)
  between operations  14.9 us (12%)
  starting transfers between devices  5.52 us (5%)
    reduce_scatter x1, waiting for transfers between devices, per_device(): fine_out = lax.psum_scatter(packed, 'blk', scatter_dimension=0, tiled=True)  46.1 us
    unnamed x58, local copies, waits for them, and re-layouts  8.76 us
    ppermute x1, starting transfers between devices, halo_rows(): high = lax.ppermute(block[:, :width], 'blk', backward)  5.03 us
    select_n x1, other arithmetic, per_device(): packed = jnp.where(send_live[:, None, None, None], fine_new[send_slot], 0.0)  4.12 us
    slice x2, local copies, waits for them, and re-layouts, average_down(): return 0.5 * (blocks[:, :, 0::2] + blocks[:, :, 1::2])  4.06 us
    slice x3, local copies, waits for them, and re-layouts, coarse_step(): face_sums = jnp.stack([speed_sum[::CB], press_sum[::CB], heat_flux[::CB]])  3.3 us
    another operation x7, local copies, waits for them, and re-layouts, coarse_step(): return (jnp.stack([pressure, velocity, warmth]), face_sums)  3.24 us
    another operation x1, other arithmetic, coarse_step(): return (jnp.stack([pressure, velocity, warmth]), face_sums)  2.7 us
  transfers between devices with their start and end apart: 3, of which 1 were waited for; matrix products, arithmetic and copies ran while one was open for 22% of the time, Pallas kernels for 0%

profile of v1, /device:TPU:0, one launch (start us, length us, event | category | flops | bytes accessed | tf_op | source)
XLA Modules:
  0.0 120.9 jit_solution(10588033360676553377)
XLA Ops:
  7.2 0.9 fusion.95
  8.6 5.0 %collective-permute-start.1 = (f32[3,8,256]{2,1,0:T(8,128)S(1)}, f32[3,8,256]{2,1,0:T(8,128)S(1)}, u32[]{:S(2)}, u32[]{:S(2)}) collective-permute-start(f32[3,8,256]{2,1,0:T(8,128)S(1)} %get-tuple-element.34), channel_id=1, source_target_pairs={{1,0},{2,1},{3,2},{4,3},{5,4},{6,5},{7,6},{8,7},{9,8},{10,9},{11,1... | collective-permute-start | bytes 73736 | tf_op jit(solution)/shard_map/ppermute | solution.py:76
  13.6 0.8 broadcast_compare_fusion
  14.7 1.3 %select_reduce_fusion.3 = s32[]{:T(128)} fusion(s32[512]{0:T(512)} %param.11, s32[]{:T(128)S(6)} %mul.240), kind=kLoop, calls=%fused_computation.255 | loop fusion | flops 1535 | bytes 2056 | tf_op jit(solution)/shard_map/reduce_sum | solution.py:103
  18.4 1.7 %slice_bitcast_fusion.5 = (f32[6,32,256]{2,1,0:T(8,128)}, f32[6,32,256]{2,1,0:T(8,128)S(1)}) fusion(f32[6,3,32,256]{3,2,1,0:T(8,128)} %param.10), kind=kLoop, calls=%fused_computation.171 | loop fusion | bytes 786432 | tf_op jit(solution)/shard_map/vmap()/squeeze | solution.py:23
  20.2 1.5 %gather_fusion = f32[12,3,256]{2,0,1:T(8,128)S(1)} fusion(f32[3,512,256]{2,1,0:T(8,128)} %param.9, s32[1024]{0:T(1024)S(1)} %pad_clamp_fusion.3), kind=kCustom, calls=%fused_computation | custom fusion | bytes 73776 | tf_op jit(solution)/shard_map/gather | solution.py:121
  23.2 0.8 copy-done.2
  24.1 1.1 fusion.8
  25.2 0.9 slice_bitcast_fusion.10
  27.4 0.8 copy-done.4
  28.3 0.8 copy-done.7
  29.5 2.7 %pad_maximum_fusion = f32[3,512,256]{2,0,1:T(4,128)} fusion(f32[1,512,256]{2,0,1:T(1,128)S(1)} %stack.79, f32[1,512,256]{2,0,1:T(1,128)S(1)} %copy.54, f32[1,512,256]{2,0,1:T(1,128)S(1)} %copy.53), kind=kLoop, calls=%fused_computation.6 | loop fusion | flops 786432 | bytes 3145728 | tf_op jit(solution)/shard_map/stack | solution.py:96
  32.2 2.2 %gather_fusion.1 = f32[12,3,256]{2,1,0:T(4,128)S(1)} fusion(f32[3,512,256]{2,0,1:T(4,128)} %pad_maximum_fusion, s32[1024]{0:T(1024)S(1)} %pad_clamp_fusion.3), kind=kCustom, calls=%fused_computation.1 | custom fusion | bytes 73776 | tf_op jit(solution)/shard_map/gather | solution.py:121
  38.0 0.7 copy-done.17
  39.5 0.7 copy-done.19
  40.4 0.7 copy-done.20
  42.2 2.4 %gather_fusion.5 = f32[32,3,32,256]{3,2,1,0:T(8,128)} fusion(f32[6,3,32,256]{3,2,1,0:T(8,128)S(1)} %maximum_bitcast_fusion, s32[1024]{0:T(1024)S(1)} %pad_clamp_fusion), kind=kCustom, calls=%fused_computation.5 | custom fusion | bytes 6291584 | tf_op jit(solution)/shard_map/gather | solution.py:127
  44.6 4.1 %broadcast_select_fusion = f32[32,3,32,256]{3,2,1,0:T(8,128)} fusion(f32[32,3,32,256]{3,2,1,0:T(8,128)} %gather_fusion.5, pred[32]{0:T(512)(128)(4,1)S(1)} %fusion.87), kind=kLoop, calls=%fused_computation.8 | loop fusion | flops 786432 | bytes 6291488 | tf_op jit(solution)/shard_map/jit(_where)/select_n | solution.py:127
  48.8 1.1 slice.807
  49.9 2.1 %slice.794 = f32[6,3,16,256]{3,2,1,0:T(8,128)} slice(f32[6,3,32,256]{3,2,1,0:T(8,128)S(1)} %maximum_bitcast_fusion), slice={[0:6:1], [0:3:1], [0:32:2], [0:256:1]} | slice | bytes 589824 | tf_op jit(solution)/shard_map/slice | solution.py:52
  52.0 1.9 %slice.795 = f32[6,3,16,256]{3,2,1,0:T(8,128)} slice(f32[6,3,32,256]{3,2,1,0:T(8,128)S(1)} %maximum_bitcast_fusion), slice={[0:6:1], [0:3:1], [1:32:2], [0:256:1]} | slice | bytes 589824 | tf_op jit(solution)/shard_map/slice | solution.py:52
  54.0 1.0 slice_add_fusion.4
  55.0 1.1 slice.806
  56.1 1.1 slice.800
  57.2 0.9 fusion.84
  58.1 1.2 %fusion.86 = (f32[1,6,256]{2,0,1:T(1,128)S(1)}, f32[1,6,256]{2,0,1:T(1,128)S(1)}) fusion(f32[6,33,256]{2,1,0:T(8,128)} %copy-done.21, f32[6,33,256]{2,1,0:T(8,128)} %copy-done.20, f32[6,33,256]{2,1,0:T(8,128)} %copy-done.19, f32[6,33,256]{2,1,0:T(8,128)} %copy-done.17, f32[6,33,256]{2,1,0:T(8,128)} %copy-done.13, f32[6,33,256]{2,1,0:T(8,128)} %copy-done.12, ...), kind=kLoop, calls=%fused_computation.230 | loop fusion | flops 21504 | bytes 110592 | tf_op jit(solution)/shard_map/vmap()/add | solution.py:38
  59.3 1.1 fusion.85
  60.6 0.8 gather_fusion.3
  61.3 1.0 add_multiply_fusion
  64.8 1.0 maximum_select_fusion
  65.9 2.1 %copy.67 = f32[3,32,16,256]{3,2,1,0:T(8,128)} copy(f32[3,32,16,256]{3,1,0,2:T(8,128)S(1)} %fusion.76) | data formatting | bytes 3145728 | tf_op jit(solution)/shard_map/scatter-add | solution.py:67
  68.0 46.1 %reduce-scatter.2.cloned.1.call-done = f32[2,3,32,256]{3,2,1,0:T(8,128)} async-done(((f32[32,3,32,256]{3,2,1,0:T(8,128)}), f32[2,3,32,256]{3,2,1,0:T(8,128)}) %reduce-scatter.2.cloned.1.call-update) | async-done | bytes 196624 | tf_op jit(solution)/shard_map/reduce_scatter | solution.py:128
  (159 shorter events, 14.4 us)
Async XLA Ops:
  7.2 9.5 %copy-start = (s32[32]{0:T(128)S(1)}, s32[32]{0:T(128)}, u32[]{:S(2)}) copy-start(s32[32]{0:T(128)} %param.12) | copy-start | bytes 388
  7.2 14.6 %copy-start.1 = (f32[3,512,256]{2,1,0:T(8,128)S(1)}, f32[3,512,256]{2,1,0:T(8,128)}, u32[]{:S(2)}) copy-start(f32[3,512,256]{2,1,0:T(8,128)} %param.9) | copy-start | bytes 4718596
  7.2 106.9 %reduce-scatter.2.cloned.1.call-start = ((), (), s32[]{:S(2)}) async-start(), calls=%async_computation.1 | async-start | bytes 3342336 | tf_op jit(solution)/shard_map/reduce_scatter | solution.py:128
  8.1 13.6 %collective-permute-start = (f32[3,8,256]{2,1,0:T(8,128)S(1)}, f32[3,8,256]{2,1,0:T(8,128)S(1)}, u32[]{:S(2)}, u32[]{:S(2)}) collective-permute-start(f32[3,8,256]{2,1,0:T(8,128)S(1)} %get-tuple-element.35), channel_id=1, source_target_pairs={{0,1},{1,2},{2,3},{3,4},{4,5},{5,6},{6,7},{7,8},{8,9},{9,10},{10,1... | collective-permute-start | bytes 73736 | tf_op jit(solution)/shard_map/ppermute | solution.py:75
  8.6 13.3 %collective-permute-start.1 = (f32[3,8,256]{2,1,0:T(8,128)S(1)}, f32[3,8,256]{2,1,0:T(8,128)S(1)}, u32[]{:S(2)}, u32[]{:S(2)}) collective-permute-start(f32[3,8,256]{2,1,0:T(8,128)S(1)} %get-tuple-element.34), channel_id=1, source_target_pairs={{1,0},{2,1},{3,2},{4,3},{5,4},{6,5},{7,6},{8,7},{9,8},{10,9},{11,1... | collective-permute-start | bytes 73736 | tf_op jit(solution)/shard_map/ppermute | solution.py:76
  23.2 0.8 copy-start.2
  26.2 1.2 %copy-start.5 = (f32[512,256]{1,0:T(8,128)}, f32[512,256]{1,0:T(8,128)S(1)}, u32[]{:S(2)}) copy-start(f32[512,256]{1,0:T(8,128)S(1)} %fusion.21) | copy-start | bytes 1572868
  27.4 0.8 copy-start.4
  28.3 0.8 copy-start.7
  29.5 5.1 %copy-start.27 = (f32[6,32,256]{2,1,0:T(8,128)S(1)}, f32[6,32,256]{2,1,0:T(8,128)}, u32[]{:S(2)}) copy-start(f32[6,32,256]{2,1,0:T(8,128)} %get-tuple-element.38) | copy-start | bytes 589828
  29.5 5.1 %copy-start.25 = (f32[6,3,32,256]{3,2,1,0:T(8,128)S(1)}, f32[6,3,32,256]{3,2,1,0:T(8,128)}, u32[]{:S(2)}) copy-start(f32[6,3,32,256]{3,2,1,0:T(8,128)} %param.10) | copy-start | bytes 1769476
  34.8 0.7 copy-start.23
  34.8 0.8 copy-start.24
  35.6 0.7 copy-start.11
  36.4 0.7 copy-start.12
  37.2 0.7 copy-start.10
  37.3 1.4 %copy-start.13 = (f32[6,33,256]{2,1,0:T(8,128)}, f32[6,33,256]{2,1,0:T(8,128)S(1)}, u32[]{:S(2)}) copy-start(f32[6,33,256]{2,1,0:T(8,128)S(1)} %fusion.45) | copy-start | bytes 608260
  37.5 1.3 %copy-start.14 = (f32[6,33,256]{2,1,0:T(8,128)}, f32[6,33,256]{2,1,0:T(8,128)S(1)}, u32[]{:S(2)}) copy-start(f32[6,33,256]{2,1,0:T(8,128)S(1)} %fusion.31) | copy-start | bytes 608260
  38.0 0.7 copy-start.17
  38.8 0.7 copy-start.15
  39.5 0.7 copy-start.19
  40.3 0.9 copy-start.16
  40.4 0.7 copy-start.20
  41.2 0.7 copy-start.18
  41.3 0.7 copy-start.21
  41.5 0.7 copy-start.22
  48.7 5.3 %copy-start.3 = (f32[515,256]{1,0:T(8,128)S(1)}, f32[515,256]{1,0:T(8,128)}, u32[]{:S(2)}) copy-start(f32[515,256]{1,0:T(8,128)} %copy-done.2) | copy-start | bytes 1582084
  54.0 7.4 %copy-start.26 = (f32[6,3,16,256]{3,2,1,0:T(8,128)S(1)}, f32[6,3,16,256]{3,2,1,0:T(8,128)}, u32[]{:S(2)}) copy-start(f32[6,3,16,256]{3,2,1,0:T(8,128)} %slice.794) | copy-start | bytes 884740
  62.4 1.1 copy-start.6
  62.4 1.4 %copy-start.9 = (f32[512,256]{1,0:T(8,128)S(1)}, f32[512,256]{1,0:T(8,128)}, u32[]{:S(2)}) copy-start(f32[512,256]{1,0:T(8,128)} %get-tuple-element.41) | copy-start | bytes 1572868
  63.1 1.1 copy-start.8
Sparse Core Ops, SparseCore 0:
  48.8 65.2 reduce-scatter.1

commit v2 on v1

v2 whole, which is shorter than its diff:
```python
import functools

import jax
import jax.numpy as jnp
from jax import lax
from jax.experimental import pallas as pl
from jax.experimental.pallas import tpu as pltpu
from jax.sharding import PartitionSpec as P

B_DEV = 32
CB = 16
FCAP = 6
FB = 32
F_DEV = 2
RIM = 8
QUAD = 4
ROWS_AT_ONCE = 64
HALF = 0.3
MESH = pl.DeviceIdType.MESH
VMEM_LIMIT = 48 * 1024 * 1024
CHUNKS = ((2, 0, 32), (0, 0, 32), (1, 0, 32))


def shifted(field):
    count = field.shape[0]
    return pltpu.roll(field, 1, 0), pltpu.roll(field, count - 1, 0)


def acoustic_substeps(pressure, velocity):
    press_sum = speed_sum = 0.0
    for substep in range(4):
        press_sum = press_sum + pressure
        below, above = shifted(pressure)
        velocity = velocity - HALF * (above - below)
        speed_sum = speed_sum + velocity
        below, above = shifted(velocity)
        pressure = pressure - HALF * (above - below)
    return pressure, velocity, press_sum, speed_sum


def heat_flux(low, high, courant):
    return 0.5 * courant * (low + high) - 0.5 * courant * courant * (high - low)


def transported(warmth, below, above, courant):
    return warmth - (heat_flux(warmth, above, courant) - heat_flux(below, warmth, courant))


def local_kernel(flags, slots, courant, coarse, fine_old, out, fine_new, table,
                 padded, fine, press_total, speed_total, pairs, where_at, sems):
    rows, columns = coarse.shape[1], coarse.shape[2]
    owners = flags.shape[0] // B_DEV
    get_coarse = pltpu.make_async_copy(coarse, padded.at[:, pl.ds(RIM, rows)], sems.at[0])
    get_coarse.start()
    get_fine = pltpu.make_async_copy(fine_old, fine, sems.at[1])
    get_fine.start()
    me = lax.axis_index("blk")

    def list_owner(owner, base):
        total = flags[owner * B_DEV]
        for at in range(1, B_DEV):
            total = total + flags[owner * B_DEV + at]

        def list_block(rank, carry):
            table[slots[base + rank]] = owner * FCAP + rank
            return carry

        lax.fori_loop(0, total, list_block, 0)
        return base + total

    lax.fori_loop(0, owners, list_owner, 0)
    count = jnp.int32(0)
    for block in range(B_DEV):
        where_at[count] = block
        count = count + flags[me * B_DEV + block]

    get_coarse.wait()
    for first in range(0, columns, 128):
        lanes = slice(first, first + 128)

        def advance(step, carry):
            start = pl.multiple_of(step * ROWS_AT_ONCE, ROWS_AT_ONCE)
            span = pl.ds(start, ROWS_AT_ONCE + 2 * RIM)
            here = pl.ds(start, ROWS_AT_ONCE)
            keep = slice(RIM, RIM + ROWS_AT_ONCE)
            results = acoustic_substeps(padded[0, span, lanes], padded[1, span, lanes])
            out[0, here, lanes] = results[0][keep]
            out[1, here, lanes] = results[1][keep]
            press_total[here, lanes] = results[2][keep]
            speed_total[here, lanes] = results[3][keep]
            warmth = padded[2, span, lanes]
            below, above = shifted(warmth)
            out[2, here, lanes] = transported(warmth, below, above, courant[:, lanes])[keep]
            return carry

        lax.fori_loop(0, rows // ROWS_AT_ONCE, advance, 0)

    get_fine.wait()
    row_at = lax.broadcasted_iota(jnp.int32, (FB, columns), 0)
    eight = lax.broadcasted_iota(jnp.int32, (RIM, columns), 0)
    number = courant[...]

    def with_edges(field, left, right):
        below, above = shifted(field)
        return (jnp.where(row_at == 0, left, below), jnp.where(row_at == FB - 1, right, above))

    def refine(slot, carry):
        begin = pl.multiple_of(where_at[slot] * CB, CB)
        before = pl.ds(begin - RIM, RIM)
        after = pl.ds(begin + CB, RIM)
        old = [(padded[f, pl.ds(begin, RIM)][RIM - 1:], padded[f, pl.ds(begin + CB + RIM, RIM)][:1])
               for f in range(3)]
        new = [(out[f, before][RIM - 1:], out[f, after][:1]) for f in range(3)]
        pressure, velocity, warmth = fine[slot, 0], fine[slot, 1], fine[slot, 2]
        regs = [[0.0, 0.0, 0.0], [0.0, 0.0, 0.0]]
        for fine_round in range(2):
            edges = [[o + 0.5 * fine_round * (n - o) for o, n in zip(old[f], new[f])] for f in range(3)]
            press_ends = [0.0, 0.0]
            speed_ends = [0.0, 0.0]
            for substep in range(4):
                press_ends = [press_ends[0] + pressure[:1], press_ends[1] + pressure[FB - 1:]]
                below, above = with_edges(pressure, *edges[0])
                velocity = velocity - HALF * (above - below)
                speed_ends = [speed_ends[0] + velocity[:1], speed_ends[1] + velocity[FB - 1:]]
                below, above = with_edges(velocity, *edges[1])
                pressure = pressure - HALF * (above - below)
            heat = [heat_flux(edges[2][0], warmth[:1], number),
                    heat_flux(warmth[FB - 1:], edges[2][1], number)]
            below, above = with_edges(warmth, *edges[2])
            warmth = transported(warmth, below, above, number)
            for side in range(2):
                regs[side][0] = regs[side][0] + HALF * (4.0 * edges[1][side] + speed_ends[side])
                regs[side][1] = regs[side][1] + HALF * (4.0 * edges[0][side] + press_ends[side])
                regs[side][2] = regs[side][2] + heat[side]
        fine_new[slot, 0] = pressure
        fine_new[slot, 1] = velocity
        fine_new[slot, 2] = warmth

        def face(total, low, high):
            return HALF * (total[pl.ds(low, RIM)][RIM - 1:] + total[pl.ds(high, RIM)][:1])

        left = [face(speed_total, begin - RIM, begin), face(press_total, begin - RIM, begin),
                heat_flux(old[2][0], padded[2, pl.ds(begin + RIM, RIM)][:1], number)]
        right = [face(speed_total, begin + RIM, begin + CB), face(press_total, begin + RIM, begin + CB),
                 heat_flux(padded[2, pl.ds(begin + CB, RIM)][RIM - 1:], old[2][1], number)]
        for f in range(3):
            out[f, before] = out[f, before] + jnp.where(eight == RIM - 1, left[f] - 0.5 * regs[0][f], 0.0)
            out[f, after] = out[f, after] - jnp.where(eight == 0, right[f] - 0.5 * regs[1][f], 0.0)
            for at in range(columns // 128):
                lanes = slice(at * 128, at * 128 + 128)
                half = pairs.at[f * (columns // 128) + at]
                half[...] = (pressure, velocity, warmth)[f][:, lanes]
                out[f, pl.ds(begin, CB), lanes] = 0.5 * (
                    half[pl.ds(0, CB, 2)] + half[pl.ds(1, CB, 2)])
        return carry

    lax.fori_loop(0, count, refine, 0)


def local_step(flags, slots, courant, coarse, fine_old):
    rows, columns = coarse.shape[1], coarse.shape[2]
    return pl.pallas_call(
        local_kernel,
        out_shape=(
            jax.ShapeDtypeStruct(coarse.shape, jnp.float32),
            jax.ShapeDtypeStruct(fine_old.shape, jnp.float32),
            jax.ShapeDtypeStruct(slots.shape, jnp.int32),
        ),
        in_specs=[
            pl.BlockSpec(memory_space=pltpu.SMEM),
            pl.BlockSpec(memory_space=pltpu.SMEM),
            pl.BlockSpec(memory_space=pltpu.VMEM),
            pl.BlockSpec(memory_space=pl.ANY),
            pl.BlockSpec(memory_space=pl.ANY),
        ],
        out_specs=(
            pl.BlockSpec(memory_space=pltpu.VMEM),
            pl.BlockSpec(memory_space=pltpu.VMEM),
            pl.BlockSpec(memory_space=pltpu.SMEM),
        ),
        scratch_shapes=[
            pltpu.VMEM((3, rows + 2 * RIM, columns), jnp.float32),
            pltpu.VMEM(fine_old.shape, jnp.float32),
            pltpu.VMEM((rows, columns), jnp.float32),
            pltpu.VMEM((rows, columns), jnp.float32),
            pltpu.VMEM((3 * (columns // 128), FB, 128), jnp.float32),
            pltpu.SMEM((B_DEV,), jnp.int32),
            pltpu.SemaphoreType.DMA((2,)),
        ],
        compiler_params=pltpu.CompilerParams(vmem_limit_bytes=VMEM_LIMIT),
        name="local_step",
    )(flags, slots, courant[None, :], coarse, fine_old)


def move_kernel(devices, table, courant, coarse, fine, moved, edges, windows, *scratch):
    parts = len(CHUNKS)
    gathered, leaving, landed = scratch[:parts], scratch[parts:2 * parts], scratch[2 * parts:3 * parts]
    core_send, core_recv, pair_send, pair_recv, pass_send, pass_recv, line_send, line_recv, rim_sems = scratch[3 * parts:]
    rows, columns = coarse.shape[1], coarse.shape[2]
    line = devices // QUAD
    group = lax.axis_index("group")
    me = lax.axis_index("blk")
    spot = lax.rem(me, QUAD)
    place = me // QUAD
    core = me + 1 - 2 * lax.rem(me, 2)
    pair = me + 2 - 4 * (spot // 2)
    up = lax.rem(me + 1, devices)
    down = lax.rem(me + devices - 1, devices)
    others = [lax.rem(me + QUAD * step, devices) for step in range(line)]

    barrier = pltpu.get_barrier_semaphore()
    greeted = [core, pair, up, down] + others[1:]
    for other in greeted:
        pl.semaphore_signal(barrier, inc=1, device_id=(group, other), device_id_type=MESH)

    inner = [
        pltpu.make_async_copy(coarse.at[:, pl.ds(0, 2 * RIM)], windows.at[0, :, pl.ds(RIM, 2 * RIM)], rim_sems.at[0]),
        pltpu.make_async_copy(coarse.at[:, pl.ds(rows - 2 * RIM, 2 * RIM)], windows.at[1, :, pl.ds(0, 2 * RIM)], rim_sems.at[1]),
    ]
    for copy in inner:
        copy.start()
    for at, (f, r, size) in enumerate(CHUNKS):
        for slot in range(FCAP):
            gathered[at][slot] = fine[slot, f, r:r + size]
    pl.semaphore_wait(barrier, len(greeted))

    def remote(source, target, send, recv, device):
        return pltpu.make_async_remote_copy(
            src_ref=source, dst_ref=target, send_sem=send, recv_sem=recv,
            device_id=(group, device), device_id_type=MESH)

    own, from_core, from_pair, from_far = [pl.ds(FCAP * at, FCAP) for at in range(QUAD)]
    to_pair, to_core, passed, along = [], [], [], []
    for at in range(parts):
        buffer = gathered[at]
        to_pair.append(remote(buffer.at[own], buffer.at[from_pair], pair_send.at[at], pair_recv.at[at], pair))
        to_core.append(remote(buffer.at[own], buffer.at[from_core], core_send.at[at], core_recv.at[at], core))
        passed.append(remote(buffer.at[from_pair], buffer.at[from_far], pass_send.at[at], pass_recv.at[at], core))
        along.append([
            remote(leaving[at].at[step - 1], landed[at].at[step],
                   line_send.at[at * line + step], line_recv.at[at * line + step], others[step])
            for step in range(1, line)])
        to_pair[at].start()
        to_core[at].start()
    rims = [
        remote(coarse.at[:, pl.ds(0, RIM)], windows.at[1, :, pl.ds(2 * RIM, RIM)], rim_sems.at[2], rim_sems.at[3], down),
        remote(coarse.at[:, pl.ds(rows - RIM, RIM)], windows.at[0, :, pl.ds(0, RIM)], rim_sems.at[4], rim_sems.at[5], up),
    ]
    for copy in rims:
        copy.start()

    def held_at(code):
        owner = code // FCAP
        theirs = lax.rem(owner, QUAD)
        low = (theirs + spot) % 2
        high = (theirs // 2 + spot // 2) % 2
        return (2 * high + low) * FCAP + code - owner * FCAP

    def send_along(at):
        for step in list(range(1, line)) + [0]:
            for t in range(F_DEV):
                value = gathered[at][held_at(table[others[step] * F_DEV + t])]
                if step:
                    leaving[at][step - 1, t] = value
                else:
                    landed[at][0, t] = value
            if step:
                along[at][step - 1].start()

    for at in range(parts + 1):
        if at < parts:
            to_pair[at].wait_recv()
            passed[at].start()
        if at >= 1:
            to_core[at - 1].wait_recv()
            passed[at - 1].wait_recv()
            send_along(at - 1)
        if at == 0:
            for copy in inner + rims:
                copy.wait()
            for side in range(2):
                keep = slice(RIM, 2 * RIM)
                put = slice(side * RIM, (side + 1) * RIM)
                results = acoustic_substeps(windows[side, 0], windows[side, 1])
                edges[0, put] = results[0][keep]
                edges[1, put] = results[1][keep]
                warmth = windows[side, 2]
                below, above = shifted(warmth)
                edges[2, put] = transported(warmth, below, above, courant[...])[keep]

    for at, (f, r, size) in enumerate(CHUNKS):
        for copy in along[at]:
            copy.wait_recv()
        for t in range(F_DEV):
            origin = table[me * F_DEV + t] // (FCAP * QUAD)
            step = (place - origin + line) % line
            moved[t, f, r:r + size] = landed[at][step, t]
    for at in range(parts):
        for copy in [to_pair[at], to_core[at], passed[at]] + along[at]:
            copy.wait_send()


def move(devices, table, courant, coarse, fine):
    columns = coarse.shape[2]
    line = devices // QUAD
    parts = len(CHUNKS)

    def per_chunk(*lead):
        return [pltpu.VMEM((*lead, size, columns), jnp.float32) for f, r, size in CHUNKS]

    dma = pltpu.SemaphoreType.DMA
    return pl.pallas_call(
        functools.partial(move_kernel, devices),
        out_shape=(
            jax.ShapeDtypeStruct((F_DEV, 3, FB, columns), jnp.float32),
            jax.ShapeDtypeStruct((3, 2 * RIM, columns), jnp.float32),
        ),
        in_specs=[
            pl.BlockSpec(memory_space=pltpu.SMEM),
            pl.BlockSpec(memory_space=pltpu.VMEM),
            pl.BlockSpec(memory_space=pl.ANY),
            pl.BlockSpec(memory_space=pltpu.VMEM),
        ],
        out_specs=(
            pl.BlockSpec(memory_space=pltpu.VMEM),
            pl.BlockSpec(memory_space=pltpu.VMEM),
        ),
        scratch_shapes=[
            pltpu.VMEM((2, 3, 3 * RIM, columns), jnp.float32),
            *per_chunk(QUAD * FCAP),
            *per_chunk(line - 1, F_DEV),
            *per_chunk(line, F_DEV),
            dma((parts,)), dma((parts,)), dma((parts,)), dma((parts,)), dma((parts,)), dma((parts,)),
            dma((parts * line,)), dma((parts * line,)), dma((6,)),
        ],
        compiler_params=pltpu.CompilerParams(
            collective_id=0, has_side_effects=True, vmem_limit_bytes=VMEM_LIMIT),
        name="move",
    )(table, courant[None, :], coarse, fine)


def per_device(devices, coarse, fine_old, refine_flags, new_slot, courant):
    coarse_out, fine_new, table = local_step(refine_flags, new_slot, courant, coarse, fine_old)
    fine_out, edges = move(devices, table, courant, coarse, fine_new)
    coarse_out = lax.dynamic_update_slice(coarse_out, edges[:, :RIM], (0, 0, 0))
    coarse_out = lax.dynamic_update_slice(
        coarse_out, edges[:, RIM:], (0, coarse.shape[1] - RIM, 0))
    return coarse_out, fine_out


def solution(mesh):
    placed = (
        P(None, ("group", "blk"), None),
        P(("group", "blk"), None, None, None),
        P("group"),
        P("group"),
        P("group"),
    )
    return jax.shard_map(
        functools.partial(per_device, mesh.shape["blk"]),
        mesh=mesh,
        in_specs=placed,
        out_specs=(P(None, ("group", "blk"), None), P(("group", "blk"), None, None, None)),
        check_vma=False,
    )
```

time: 122 us -> 48.2 us (0.40)
  waiting for transfers between devices: 46.1 us -> 0 us
  Pallas kernels: 0 us -> 40.3 us
  local copies, waits for them, and re-layouts: 32.7 us -> 6.38 us
  other arithmetic: 21.6 us -> 0 us
  between operations: 14.9 us -> 0.67 us
  starting transfers between devices: 5.52 us -> 0 us
    reduce_scatter x1 -> x0, waiting for transfers between devices: 46.1 us -> none  [per_device(): fine_out = lax.psum_scatter(packed, 'blk', scatter_dimension=0, tiled=True)]
    pallas_call x0 -> x2, Pallas kernels: none -> 40.3 us  [the longest x1 35.7 us: move(): pl.pallas_call(functools.partial(move_kernel, devices), out_shape=(jax.Sh...]
    slice x13 -> x0, local copies, waits for them, and re-layouts: 8.54 us -> none  [the longest x2 4.06 us: average_down(): return 0.5 * (blocks[:, :, 0::2] + blocks[:, :, 1::2])]
    gather x8 -> x0, local copies, waits for them, and re-layouts: 8.19 us -> none  [the longest x1 2.38 us: per_device(): packed = jnp.where(send_live[:, None, None, None], fine_new[send_slot], 0.0)]
    select_n x7 -> x0, other arithmetic: 5.91 us -> none  [the longest x1 4.12 us: per_device(): packed = jnp.where(send_live[:, None, None, None], fine_new[send_slot], 0.0)]
    ppermute x2 -> x0, starting transfers between devices: 5.49 us -> none  [the longest x1 5.03 us: halo_rows(): high = lax.ppermute(block[:, :width], 'blk', backward)]
    add x6 -> x0, other arithmetic: 5.37 us -> none  [the longest x1 1.24 us: fine_steps(): flux_left[0] + speed_flux[0]]
    unnamed x58 -> x13, local copies, waits for them, and re-layouts: 8.76 us -> 5.16 us
  transfers between devices with their start and end apart: 3 -> 0, of which waited for: 1 -> 0; matrix products, arithmetic and copies ran while one was open for 22% -> 0% of each run, Pallas kernels for 0% -> 0%
where the time goes in v2:
time: 48.2 us; the launch traced here: 47.3 us
  Pallas kernels  40.3 us (84%)
  local copies, waits for them, and re-layouts  6.38 us (13%)
  between operations  0.67 us (1%)
    pallas_call x1, Pallas kernels, move(): pl.pallas_call(functools.partial(move_kernel, devices), out_shape=(jax.Sh...  35.7 us
    unnamed x13, local copies, waits for them, and re-layouts  5.16 us
    pallas_call x1, Pallas kernels, local_step(): pl.pallas_call(local_kernel, out_shape=(jax.ShapeDtypeStruct(coarse.shape...  4.51 us

profile of v2, /device:TPU:0, one launch (start us, length us, event | category | flops | bytes accessed | tf_op | source)
XLA Modules:
  0.0 47.3 jit_solution(3058549292689927906)
XLA Ops:
  0.6 0.0 copy-start
  0.6 1.4 %copy-done = f32[3,512,256]{2,1,0:T(8,128)S(1)} copy-done((f32[3,512,256]{2,1,0:T(8,128)S(1)}, f32[3,512,256]{2,1,0:T(8,128)}, u32[]{:S(2)}) %copy-start) | copy-done | bytes 1572888
  2.0 0.0 copy-start.2
  2.0 1.1 %copy-done.2 = f32[6,3,32,256]{3,2,1,0:T(8,128)S(1)} copy-done((f32[6,3,32,256]{3,2,1,0:T(8,128)S(1)}, f32[6,3,32,256]{3,2,1,0:T(8,128)}, u32[]{:S(2)}) %copy-start.2) | copy-done | bytes 589848
  3.1 0.0 copy-start.3
  3.1 0.7 %copy-done.3 = f32[256]{0:T(256)S(1)} copy-done((f32[256]{0:T(256)S(1)}, f32[256]{0:T(256)}, u32[]{:S(2)}) %copy-start.3) | copy-done | bytes 1048
  3.8 0.0 copy-start.4
  3.8 0.7 %copy-done.4 = s32[512]{0:T(512)S(1)} copy-done((s32[512]{0:T(512)S(1)}, s32[512]{0:T(512)}, u32[]{:S(2)}) %copy-start.4) | copy-done | bytes 2072
  4.5 0.0 copy-start.5
  4.5 0.7 %copy-done.5 = s32[32]{0:T(128)S(1)} copy-done((s32[32]{0:T(128)S(1)}, s32[32]{0:T(128)}, u32[]{:S(2)}) %copy-start.5) | copy-done | bytes 152
  5.1 0.0 copy-start.1
  5.1 4.5 %local_step.1 = (f32[3,512,256]{2,1,0:T(8,128)}, f32[6,3,32,256]{3,2,1,0:T(8,128)S(1)}, s32[32]{0:T(128)S(1)}) custom-call(s32[512]{0:T(512)S(1)} %copy-done.4, s32[32]{0:T(128)S(1)} %copy-done.5, f32[1,256]{1,0:T(1,128)S(1)} %bitcast.1, f32[3,512,256]{2,1,0:T(8,128)S(1)} %copy-done, f32[6,3,32,256]{3,2,1,0:T(8,128)S(1)} %copy-done.2), custom_call_target="tpu_custom_call" | custom-call | tf_op jit(solution)/shard_map/local_step/pallas_call | solution.py:162
  9.6 0.0 copy-done.1
  9.7 35.7 %move.1 = (f32[2,3,32,256]{3,2,1,0:T(8,128)S(1)}, f32[3,16,256]{2,1,0:T(8,128)S(1)}) custom-call(s32[32]{0:T(128)S(1)} %get-tuple-element.8.table, f32[1,256]{1,0:T(1,128)S(1)} %bitcast.2, f32[3,512,256]{2,1,0:T(8,128)S(1)} %copy-done.1, f32[6,3,32,256]{3,2,1,0:T(8,128)S(1)} %get-tuple-element.9.fine), custom_call_target="tpu_custom_call" | custom-call | tf_op jit(solution)/shard_map/move/pallas_call | solution.py:312
  45.4 0.6 %slice_dynamic-update-slice_fusion.1 = f32[3,512,256]{2,1,0:T(8,128)} fusion(f32[3,512,256]{2,1,0:T(8,128)} %get-tuple-element.7, f32[3,16,256]{2,1,0:T(8,128)S(1)} %get-tuple-element.10), kind=kLoop, calls=%fused_computation.1 | loop fusion | bytes 49152 | tf_op jit(solution)/shard_map/dynamic_update_slice | solution.py:345
  46.0 0.6 %slice_dynamic-update-slice_fusion = f32[3,512,256]{2,1,0:T(8,128)} fusion(f32[3,512,256]{2,1,0:T(8,128)} %slice_dynamic-update-slice_fusion.1, f32[3,16,256]{2,1,0:T(8,128)S(1)} %get-tuple-element.10), kind=kLoop, calls=%fused_computation | loop fusion | bytes 49152 | tf_op jit(solution)/shard_map/dynamic_update_slice | solution.py:346
  46.6 0.7 %copy.10 = f32[2,3,32,256]{3,2,1,0:T(8,128)} copy(f32[2,3,32,256]{3,2,1,0:T(8,128)S(1)} %get-tuple-element.15) | data formatting | bytes 393216
Async XLA Ops:
  0.6 1.4 %copy-start = (f32[3,512,256]{2,1,0:T(8,128)S(1)}, f32[3,512,256]{2,1,0:T(8,128)}, u32[]{:S(2)}) copy-start(f32[3,512,256]{2,1,0:T(8,128)} %coarse.3) | copy-start | bytes 4718596
  2.0 1.1 %copy-start.2 = (f32[6,3,32,256]{3,2,1,0:T(8,128)S(1)}, f32[6,3,32,256]{3,2,1,0:T(8,128)}, u32[]{:S(2)}) copy-start(f32[6,3,32,256]{3,2,1,0:T(8,128)} %fine_old.1) | copy-start | bytes 1769476
  3.1 0.7 %copy-start.3 = (f32[256]{0:T(256)S(1)}, f32[256]{0:T(256)}, u32[]{:S(2)}) copy-start(f32[256]{0:T(256)} %param.9) | copy-start | bytes 3076
  3.8 0.7 %copy-start.4 = (s32[512]{0:T(512)S(1)}, s32[512]{0:T(512)}, u32[]{:S(2)}) copy-start(s32[512]{0:T(512)} %flags.1) | copy-start | bytes 6148
  4.5 0.7 %copy-start.5 = (s32[32]{0:T(128)S(1)}, s32[32]{0:T(128)}, u32[]{:S(2)}) copy-start(s32[32]{0:T(128)} %slots.1) | copy-start | bytes 388
  5.1 4.5 %copy-start.1 = (f32[3,512,256]{2,1,0:T(8,128)S(1)}, f32[3,512,256]{2,1,0:T(8,128)}, u32[]{:S(2)}) copy-start(f32[3,512,256]{2,1,0:T(8,128)} %coarse.3) | copy-start | bytes 4718596

commit v3 on v2

v3 whole, which is shorter than its diff:
```python
import functools

import jax
import jax.numpy as jnp
from jax import lax
from jax.experimental import pallas as pl
from jax.experimental.pallas import tpu as pltpu
from jax.sharding import PartitionSpec as P

B_DEV = 32
CB = 16
FCAP = 6
FB = 32
F_DEV = 2
RIM = 8
QUAD = 4
ROWS_AT_ONCE = 64
PARENTS = 8
HALF = 0.3
MESH = pl.DeviceIdType.MESH
VMEM_LIMIT = 48 * 1024 * 1024
CHUNKS = ((2, 0, 16), (2, 16, 16), (0, 0, 16), (0, 16, 16), (1, 0, 16), (1, 16, 16))


def shifted(field):
    count = field.shape[0]
    return pltpu.roll(field, 1, 0), pltpu.roll(field, count - 1, 0)


def acoustic_substeps(pressure, velocity):
    press_sum = speed_sum = 0.0
    for substep in range(4):
        press_sum = press_sum + pressure
        below, above = shifted(pressure)
        velocity = velocity - HALF * (above - below)
        speed_sum = speed_sum + velocity
        below, above = shifted(velocity)
        pressure = pressure - HALF * (above - below)
    return pressure, velocity, press_sum, speed_sum


def heat_flux(low, high, courant):
    return 0.5 * courant * (low + high) - 0.5 * courant * courant * (high - low)


def transported(warmth, below, above, courant):
    return warmth - (heat_flux(warmth, above, courant) - heat_flux(below, warmth, courant))


def plan_kernel(flags_at, slots_at, plan, flags, slots, sems):
    get_flags = pltpu.make_async_copy(flags_at, flags, sems.at[0])
    get_slots = pltpu.make_async_copy(slots_at, slots, sems.at[1])
    get_flags.start()
    get_slots.start()
    get_flags.wait()
    get_slots.wait()
    me = lax.axis_index("blk")
    owners = flags.shape[0] // B_DEV
    fine_count = slots.shape[0]

    def list_owner(owner, base):
        total = flags[owner * B_DEV]
        for at in range(1, B_DEV):
            total = total + flags[owner * B_DEV + at]

        def list_block(rank, carry):
            plan[slots[base + rank]] = owner * FCAP + rank
            return carry

        lax.fori_loop(0, total, list_block, 0)
        return base + total

    lax.fori_loop(0, owners, list_owner, 0)
    for slot in range(PARENTS):
        plan[fine_count + slot] = 0
    ranks = fine_count + PARENTS + 1
    plan[ranks - 1] = FCAP
    plan[ranks + B_DEV] = FCAP
    count = jnp.int32(0)
    for block in range(1, B_DEV - 1):
        flag = flags[me * B_DEV + block]
        before = plan[fine_count + count]
        plan[fine_count + count] = jnp.where(flag == 1, block - 1, before)
        plan[ranks + block] = jnp.where(flag == 1, count, FCAP)
        count = count + flag
    plan[ranks] = FCAP
    plan[ranks + B_DEV - 1] = FCAP


def make_plan(flags, slots):
    return pl.pallas_call(
        plan_kernel,
        out_shape=jax.ShapeDtypeStruct((slots.shape[0] + PARENTS + B_DEV + 2,), jnp.int32),
        in_specs=[pl.BlockSpec(memory_space=pltpu.HBM)] * 2,
        out_specs=pl.BlockSpec(memory_space=pltpu.SMEM),
        scratch_shapes=[
            pltpu.SMEM(flags.shape, jnp.int32),
            pltpu.SMEM(slots.shape, jnp.int32),
            pltpu.SemaphoreType.DMA((2,)),
        ],
        name="make_plan",
    )(flags, slots)


def step_kernel(devices, plan, courant, coarse, fine, out, moved,
                windows, blocks, averages, fixes, halves, *scratch):
    parts = len(CHUNKS)
    gathered, leaving, landed = scratch[:parts], scratch[parts:2 * parts], scratch[2 * parts:3 * parts]
    core_send, core_recv, pair_send, pair_recv, pass_send, pass_recv, line_send, line_recv, rim_sems = scratch[3 * parts:]
    rows, columns = coarse.shape[1], coarse.shape[2]
    fine_count = devices * F_DEV
    line = devices // QUAD
    group = lax.axis_index("group")
    me = lax.axis_index("blk")
    spot = lax.rem(me, QUAD)
    place = me // QUAD
    core = me + 1 - 2 * lax.rem(me, 2)
    pair = me + 2 - 4 * (spot // 2)
    up = lax.rem(me + 1, devices)
    down = lax.rem(me + devices - 1, devices)
    others = [lax.rem(me + QUAD * step, devices) for step in range(line)]

    barrier = pltpu.get_barrier_semaphore()
    greeted = [core, pair, up, down] + others[1:]
    for other in greeted:
        pl.semaphore_signal(barrier, inc=1, device_id=(group, other), device_id_type=MESH)

    averages[FCAP] = jnp.zeros(averages.shape[1:], jnp.float32)
    fixes[FCAP] = jnp.zeros(fixes.shape[1:], jnp.float32)

    def copy_block(block, carry):
        for f in range(3):
            blocks[block, f] = coarse[f, pl.ds(pl.multiple_of(block * CB, CB), CB)]
        return carry

    lax.fori_loop(0, B_DEV, copy_block, 0)

    def remote(source, target, send, recv, device):
        return pltpu.make_async_remote_copy(
            src_ref=source, dst_ref=target, send_sem=send, recv_sem=recv,
            device_id=(group, device), device_id_type=MESH)

    own, from_core, from_pair, from_far = [pl.ds(FCAP * at, FCAP) for at in range(QUAD)]
    to_pair, to_core, passed, along = [], [], [], []
    for at in range(parts):
        buffer = gathered[at]
        to_pair.append(remote(buffer.at[own], buffer.at[from_pair], pair_send.at[at], pair_recv.at[at], pair))
        to_core.append(remote(buffer.at[own], buffer.at[from_core], core_send.at[at], core_recv.at[at], core))
        passed.append(remote(buffer.at[from_pair], buffer.at[from_far], pass_send.at[at], pass_recv.at[at], core))
        along.append([
            remote(leaving[at].at[step - 1], landed[at].at[step],
                   line_send.at[at * line + step], line_recv.at[at * line + step], others[step])
            for step in range(1, line)])
    rims = [
        remote(coarse.at[:, pl.ds(0, RIM)], windows.at[1, :, pl.ds(2 * RIM, RIM)], rim_sems.at[0], rim_sems.at[1], down),
        remote(coarse.at[:, pl.ds(rows - RIM, RIM)], windows.at[0, :, pl.ds(0, RIM)], rim_sems.at[2], rim_sems.at[3], up),
    ]

    number = courant[...]
    row_at = lax.broadcasted_iota(jnp.int32, (FB, columns), 0)
    eight = lax.broadcasted_iota(jnp.int32, (RIM, columns), 0)

    def with_edges(field, left, right):
        below, above = shifted(field)
        return (jnp.where(row_at == 0, left, below), jnp.where(row_at == FB - 1, right, above))

    def around(slot, f):
        block = plan[fine_count + slot]
        return jnp.concatenate([blocks[block, f], blocks[block + 1, f], blocks[block + 2, f]], 0)

    def ghosts(old, new):
        pairs = [(old[CB - 1:CB], new[CB - 1:CB]), (old[2 * CB:2 * CB + 1], new[2 * CB:2 * CB + 1])]
        return [[o + 0.5 * fine_round * (n - o) for o, n in pairs] for fine_round in range(2)]

    def face(total):
        return [HALF * (total[CB - 1:CB] + total[CB:CB + 1]),
                HALF * (total[2 * CB - 1:2 * CB] + total[2 * CB:2 * CB + 1])]

    def keep_block(slot, f, value, faces, regs):
        for at, (field, r, size) in enumerate(CHUNKS):
            if field == f:
                gathered[at][slot] = value[r:r + size]
        fixes[slot, 0, f] = jnp.where(eight == RIM - 1, faces[0] - 0.5 * regs[0], 0.0)
        fixes[slot, 1, f] = jnp.where(eight == 0, 0.5 * regs[1] - faces[1], 0.0)
        for at in range(columns // 128):
            lanes = slice(at * 128, at * 128 + 128)
            half = halves.at[slot, f, at]
            half[...] = value[:, lanes]
            averages[slot, f, :, lanes] = 0.5 * (half[pl.ds(0, CB, 2)] + half[pl.ds(1, CB, 2)])

    def refine_warmth(slot):
        old = around(slot, 2)
        below, above = shifted(old)
        edges = ghosts(old, transported(old, below, above, number))
        warmth = fine[slot, 2]
        regs = [0.0, 0.0]
        for left, right in edges:
            regs = [regs[0] + heat_flux(left, warmth[:1], number),
                    regs[1] + heat_flux(warmth[FB - 1:], right, number)]
            below, above = with_edges(warmth, left, right)
            warmth = transported(warmth, below, above, number)
        faces = [heat_flux(old[at - 1:at], old[at:at + 1], number) for at in (CB, 2 * CB)]
        keep_block(slot, 2, warmth, faces, regs)

    def refine_sound(slot):
        old_press, old_speed = around(slot, 0), around(slot, 1)
        new_press, new_speed, press_total, speed_total = acoustic_substeps(old_press, old_speed)
        press_edges, speed_edges = ghosts(old_press, new_press), ghosts(old_speed, new_speed)
        pressure, velocity = fine[slot, 0], fine[slot, 1]
        press_regs, speed_regs = [0.0, 0.0], [0.0, 0.0]
        for press_ends, speed_ends in zip(press_edges, speed_edges):
            press_sums, speed_sums = [4.0 * end for end in press_ends], [4.0 * end for end in speed_ends]
            for substep in range(4):
                press_sums = [press_sums[0] + pressure[:1], press_sums[1] + pressure[FB - 1:]]
                below, above = with_edges(pressure, *press_ends)
                velocity = velocity - HALF * (above - below)
                speed_sums = [speed_sums[0] + velocity[:1], speed_sums[1] + velocity[FB - 1:]]
                below, above = with_edges(velocity, *speed_ends)
                pressure = pressure - HALF * (above - below)
            press_regs = [reg + HALF * total for reg, total in zip(press_regs, press_sums)]
            speed_regs = [reg + HALF * total for reg, total in zip(speed_regs, speed_sums)]
        keep_block(slot, 0, pressure, face(speed_total), speed_regs)
        keep_block(slot, 1, velocity, face(press_total), press_regs)

    def each_pair(work):
        def two(at, carry):
            work(2 * at)
            work(2 * at + 1)
            return carry

        lax.fori_loop(0, FCAP // 2, two, 0)

    def bulk(load_from, store_to, skip):
        for first in range(0, columns, 128):
            lanes = slice(first, first + 128)
            span = pl.ds(load_from, ROWS_AT_ONCE + 2 * RIM)
            here = pl.ds(store_to, ROWS_AT_ONCE)
            keep = slice(skip, skip + ROWS_AT_ONCE)
            results = acoustic_substeps(coarse[0, span, lanes], coarse[1, span, lanes])
            out[0, here, lanes] = results[0][keep]
            out[1, here, lanes] = results[1][keep]
            warmth = coarse[2, span, lanes]
            below, above = shifted(warmth)
            out[2, here, lanes] = transported(warmth, below, above, number[:, lanes])[keep]

    pieces = rows // ROWS_AT_ONCE

    def bulk_some(low, high):
        def one(at, carry):
            start = pl.multiple_of(at * ROWS_AT_ONCE, ROWS_AT_ONCE)
            bulk(start - RIM, start, RIM)
            return carry

        lax.fori_loop(low, high, one, 0)

    def bulk_ends():
        bulk(0, 0, 0)
        bulk(rows - ROWS_AT_ONCE - 2 * RIM, rows - ROWS_AT_ONCE, 2 * RIM)

    def outer_rows():
        windows[0, :, RIM:] = coarse[:, :2 * RIM]
        windows[1, :, :2 * RIM] = coarse[:, rows - 2 * RIM:]
        for copy in rims:
            copy.wait()
        for side in range(2):
            keep = slice(RIM, 2 * RIM)
            put = slice(0, RIM) if side == 0 else slice(rows - RIM, rows)
            results = acoustic_substeps(windows[side, 0], windows[side, 1])
            out[0, put] = results[0][keep]
            out[1, put] = results[1][keep]
            warmth = windows[side, 2]
            below, above = shifted(warmth)
            out[2, put] = transported(warmth, below, above, number)[keep]

    def merge_fine():
        ranks = fine_count + PARENTS + 1

        def one(block, carry):
            before, here, after = [plan[ranks + block + at] for at in (-1, 0, 1)]
            low = pl.ds(pl.multiple_of(block * CB, CB), RIM)
            high = pl.ds(pl.multiple_of(block * CB + RIM, RIM), RIM)
            refined = jnp.full((RIM, columns), here, jnp.int32) < FCAP
            for f in range(3):
                mean = averages[here, f]
                out[f, low] = jnp.where(refined, mean[:RIM], out[f, low] + fixes[before, 1, f])
                out[f, high] = jnp.where(refined, mean[RIM:], out[f, high] + fixes[after, 0, f])
            return carry

        lax.fori_loop(0, B_DEV, one, 0)

    def held_at(code):
        owner = code // FCAP
        theirs = lax.rem(owner, QUAD)
        low = (theirs + spot) % 2
        high = (theirs // 2 + spot // 2) % 2
        return (2 * high + low) * FCAP + code - owner * FCAP

    def send_along(at):
        for step in list(range(1, line)) + [0]:
            for t in range(F_DEV):
                value = gathered[at][held_at(plan[others[step] * F_DEV + t])]
                if step:
                    leaving[at][step - 1, t] = value
                else:
                    landed[at][0, t] = value
            if step:
                along[at][step - 1].start()

    warm_parts = sum(f == 2 for f, r, size in CHUNKS)
    each_pair(refine_warmth)
    pl.semaphore_wait(barrier, len(greeted))
    for at in range(warm_parts):
        to_core[at].start()
        to_pair[at].start()
    each_pair(refine_sound)
    for copy in rims:
        copy.start()
    for at in range(warm_parts, parts):
        to_core[at].start()
    work = [lambda: bulk_some(1, 3), lambda: bulk_some(3, 5), lambda: bulk_some(5, pieces - 1),
            bulk_ends, outer_rows, merge_fine]
    for at in range(parts + 1):
        if at < parts:
            to_pair[at].wait_recv()
            passed[at].start()
            to_pair[at].wait_send()
            if at + warm_parts < parts:
                to_pair[at + warm_parts].start()
        if at >= 1:
            to_core[at - 1].wait_recv()
            passed[at - 1].wait_recv()
            send_along(at - 1)
            work[at - 1]()

    for at, (f, r, size) in enumerate(CHUNKS):
        for copy in along[at]:
            copy.wait_recv()
        for t in range(F_DEV):
            origin = plan[me * F_DEV + t] // (FCAP * QUAD)
            step = (place - origin + line) % line
            moved[t, f, r:r + size] = landed[at][step, t]
    for at in range(parts):
        for copy in [to_core[at], passed[at]] + along[at]:
            copy.wait_send()


def whole_step(devices, plan, courant, coarse, fine):
    columns = coarse.shape[2]
    line = devices // QUAD
    parts = len(CHUNKS)

    def per_chunk(*lead):
        return [pltpu.VMEM((*lead, size, columns), jnp.float32) for f, r, size in CHUNKS]

    dma = pltpu.SemaphoreType.DMA
    vmem = pl.BlockSpec(memory_space=pltpu.VMEM)
    return pl.pallas_call(
        functools.partial(step_kernel, devices),
        out_shape=(
            jax.ShapeDtypeStruct(coarse.shape, jnp.float32),
            jax.ShapeDtypeStruct((F_DEV, 3, FB, columns), jnp.float32),
        ),
        in_specs=[pl.BlockSpec(memory_space=pltpu.SMEM), vmem, vmem, vmem],
        out_specs=(vmem, vmem),
        scratch_shapes=[
            pltpu.VMEM((2, 3, 3 * RIM, columns), jnp.float32),
            pltpu.VMEM((B_DEV, 3, CB, columns), jnp.float32),
            pltpu.VMEM((FCAP + 1, 3, CB, columns), jnp.float32),
            pltpu.VMEM((FCAP + 1, 2, 3, RIM, columns), jnp.float32),
            pltpu.VMEM((FCAP, 3, columns // 128, FB, 128), jnp.float32),
            *per_chunk(QUAD * FCAP),
            *per_chunk(line - 1, F_DEV),
            *per_chunk(line, F_DEV),
            dma((parts,)), dma((parts,)), dma((parts,)), dma((parts,)), dma((parts,)), dma((parts,)),
            dma((parts * line,)), dma((parts * line,)), dma((4,)),
        ],
        compiler_params=pltpu.CompilerParams(
            collective_id=0, has_side_effects=True, vmem_limit_bytes=VMEM_LIMIT),
        name="whole_step",
    )(plan, courant[None, :], coarse, fine)


def per_device(devices, coarse, fine_old, refine_flags, new_slot, courant):
    plan = make_plan(refine_flags, new_slot)
    return whole_step(devices, plan, courant, coarse, fine_old)


def solution(mesh):
    placed = (
        P(None, ("group", "blk"), None),
        P(("group", "blk"), None, None, None),
        P("group"),
        P("group"),
        P("group"),
    )
    return jax.shard_map(
        functools.partial(per_device, mesh.shape["blk"]),
        mesh=mesh,
        in_specs=placed,
        out_specs=(P(None, ("group", "blk"), None), P(("group", "blk"), None, None, None)),
        check_vma=False,
    )
```

time: 48.2 us -> 39.8 us (0.83); the launches traced: 47.3 us -> 39.5 us
  Pallas kernels: 40.3 us -> 33.2 us
  local copies, waits for them, and re-layouts: 6.38 us -> 5.62 us
    pallas_call x2, Pallas kernels: 40.3 us -> 33.2 us  [the longest x1 31.1 us: whole_step(): pl.pallas_call(functools.partial(step_kernel, devices), out_shape=(jax.Sh...]
    dynamic_update_slice x2 -> x0, local copies, waits for them, and re-layouts: 1.22 us -> none  [the longest x1 0.61 us: per_device(): coarse_out = lax.dynamic_update_slice(coarse_out, edges[:, :RIM], (0, 0, 0))]
    unnamed x13 -> x10, local copies, waits for them, and re-layouts: 5.16 us -> 5.62 us
where the time goes in v3:
time: 39.8 us; the launch traced here: 39.5 us
  Pallas kernels  33.2 us (83%)
  local copies, waits for them, and re-layouts  5.62 us (14%)
  between operations  0.66 us (2%)
    pallas_call x1, Pallas kernels, whole_step(): pl.pallas_call(functools.partial(step_kernel, devices), out_shape=(jax.Sh...  31.1 us
    unnamed x10, local copies, waits for them, and re-layouts  5.62 us
    pallas_call x1, Pallas kernels, make_plan(): pl.pallas_call(plan_kernel, out_shape=jax.ShapeDtypeStruct((slots.shape[0...  2.13 us

profile of v3, /device:TPU:0, one launch (start us, length us, event | category | flops | bytes accessed | tf_op | source)
XLA Modules:
  0.0 39.5 jit_solution(14575052966256062009)
XLA Ops:
  0.6 2.1 %make_plan.1.plan = s32[74]{0:T(128)} custom-call(s32[512]{0:T(512)} %flags_at.1, s32[32]{0:T(128)} %slots_at.1), custom_call_target="tpu_custom_call" | custom-call | tf_op jit(solution)/shard_map/make_plan/pallas_call | solution.py:91
  2.8 0.0 copy-start
  2.8 1.4 %copy-done = f32[3,512,256]{2,1,0:T(8,128)S(1)} copy-done((f32[3,512,256]{2,1,0:T(8,128)S(1)}, f32[3,512,256]{2,1,0:T(8,128)}, u32[]{:S(2)}) %copy-start) | copy-done | bytes 1572888
  4.2 0.0 copy-start.1
  4.2 1.1 %copy-done.1 = f32[6,3,32,256]{3,2,1,0:T(8,128)S(1)} copy-done((f32[6,3,32,256]{3,2,1,0:T(8,128)S(1)}, f32[6,3,32,256]{3,2,1,0:T(8,128)}, u32[]{:S(2)}) %copy-start.1) | copy-done | bytes 589848
  5.2 0.0 copy-start.2
  5.2 0.7 %copy-done.2 = s32[74]{0:T(128)S(1)} copy-done((s32[74]{0:T(128)S(1)}, s32[74]{0:T(128)}, u32[]{:S(2)}) %copy-start.2) | copy-done | bytes 320
  5.9 0.0 copy-start.3
  5.9 0.7 %copy-done.3 = f32[256]{0:T(256)S(1)} copy-done((f32[256]{0:T(256)S(1)}, f32[256]{0:T(256)}, u32[]{:S(2)}) %copy-start.3) | copy-done | bytes 1048
  6.6 31.1 %whole_step.1 = (f32[3,512,256]{2,1,0:T(8,128)S(1)}, f32[2,3,32,256]{3,2,1,0:T(8,128)S(1)}) custom-call(s32[74]{0:T(128)S(1)} %copy-done.2, f32[1,256]{1,0:T(1,128)S(1)} %bitcast.1, f32[3,512,256]{2,1,0:T(8,128)S(1)} %copy-done, f32[6,3,32,256]{3,2,1,0:T(8,128)S(1)} %copy-done.1), custom_call_target="tpu_custom_call" | custom-call | tf_op jit(solution)/shard_map/whole_step/pallas_call | solution.py:357
  37.7 1.1 %copy.9 = f32[3,512,256]{2,1,0:T(8,128)} copy(f32[3,512,256]{2,1,0:T(8,128)S(1)} %get-tuple-element.4) | data formatting | bytes 3145728
  38.8 0.7 %copy.10 = f32[2,3,32,256]{3,2,1,0:T(8,128)} copy(f32[2,3,32,256]{3,2,1,0:T(8,128)S(1)} %get-tuple-element.5) | data formatting | bytes 393216
Async XLA Ops:
  2.8 1.4 %copy-start = (f32[3,512,256]{2,1,0:T(8,128)S(1)}, f32[3,512,256]{2,1,0:T(8,128)}, u32[]{:S(2)}) copy-start(f32[3,512,256]{2,1,0:T(8,128)} %coarse.1) | copy-start | bytes 4718596
  4.2 1.1 %copy-start.1 = (f32[6,3,32,256]{3,2,1,0:T(8,128)S(1)}, f32[6,3,32,256]{3,2,1,0:T(8,128)}, u32[]{:S(2)}) copy-start(f32[6,3,32,256]{3,2,1,0:T(8,128)} %fine.1) | copy-start | bytes 1769476
  5.2 0.7 %copy-start.2 = (s32[74]{0:T(128)S(1)}, s32[74]{0:T(128)}, u32[]{:S(2)}) copy-start(s32[74]{0:T(128)} %make_plan.1.plan) | copy-start | bytes 892
  5.9 0.7 %copy-start.3 = (f32[256]{0:T(256)S(1)}, f32[256]{0:T(256)}, u32[]{:S(2)}) copy-start(f32[256]{0:T(256)} %param.9) | copy-start | bytes 3076

commit v4 on v3

--- a/solution.py
+++ b/solution.py
@@ -18,8 +18,9 @@
 PARENTS = 8
 HALF = 0.3
 MESH = pl.DeviceIdType.MESH
-VMEM_LIMIT = 48 * 1024 * 1024
+VMEM_LIMIT = 64 * 1024 * 1024
 CHUNKS = ((2, 0, 16), (2, 16, 16), (0, 0, 16), (0, 16, 16), (1, 0, 16), (1, 16, 16))
+AHEAD = 2
 
 
 def shifted(field):
@@ -102,8 +103,9 @@
     )(flags, slots)
 
 
-def step_kernel(devices, plan, courant, coarse, fine, out, moved,
-                windows, blocks, averages, fixes, halves, *scratch):
+def step_kernel(devices, plan, courant_at, coarse_at, blocks_at, fine_at, out, moved,
+                courant, coarse, press_blocks, speed_blocks, warm_blocks, fine, fetch_sems,
+                windows, averages, fixes, halves, *scratch):
     parts = len(CHUNKS)
     gathered, leaving, landed = scratch[:parts], scratch[parts:2 * parts], scratch[2 * parts:3 * parts]
     core_send, core_recv, pair_send, pair_recv, pass_send, pass_recv, line_send, line_recv, rim_sems = scratch[3 * parts:]
@@ -128,12 +130,16 @@
     averages[FCAP] = jnp.zeros(averages.shape[1:], jnp.float32)
     fixes[FCAP] = jnp.zeros(fixes.shape[1:], jnp.float32)
 
-    def copy_block(block, carry):
-        for f in range(3):
-            blocks[block, f] = coarse[f, pl.ds(pl.multiple_of(block * CB, CB), CB)]
-        return carry
-
-    lax.fori_loop(0, B_DEV, copy_block, 0)
+    blocks = (press_blocks, speed_blocks, warm_blocks)
+    fetched = [
+        pltpu.make_async_copy(source, target, fetch_sems.at[at])
+        for at, (source, target) in enumerate([
+            (courant_at, courant), (blocks_at.at[2], warm_blocks),
+            (fine_at.at[:, pl.ds(2, 1)], fine.at[:, pl.ds(2, 1)]),
+            (blocks_at.at[0], press_blocks), (blocks_at.at[1], speed_blocks),
+            (fine_at.at[:, pl.ds(0, 2)], fine.at[:, pl.ds(0, 2)]), (coarse_at, coarse)])]
+    for copy in fetched:
+        copy.start()
 
     def remote(source, target, send, recv, device):
         return pltpu.make_async_remote_copy(
@@ -152,10 +158,12 @@
                    line_send.at[at * line + step], line_recv.at[at * line + step], others[step])
             for step in range(1, line)])
     rims = [
-        remote(coarse.at[:, pl.ds(0, RIM)], windows.at[1, :, pl.ds(2 * RIM, RIM)], rim_sems.at[0], rim_sems.at[1], down),
-        remote(coarse.at[:, pl.ds(rows - RIM, RIM)], windows.at[0, :, pl.ds(0, RIM)], rim_sems.at[2], rim_sems.at[3], up),
+        remote(coarse_at.at[:, pl.ds(0, RIM)], windows.at[1, :, pl.ds(2 * RIM, RIM)], rim_sems.at[0], rim_sems.at[1], down),
+        remote(coarse_at.at[:, pl.ds(rows - RIM, RIM)], windows.at[0, :, pl.ds(0, RIM)], rim_sems.at[2], rim_sems.at[3], up),
     ]
 
+    for copy in fetched[:3]:
+        copy.wait()
     number = courant[...]
     row_at = lax.broadcasted_iota(jnp.int32, (FB, columns), 0)
     eight = lax.broadcasted_iota(jnp.int32, (RIM, columns), 0)
@@ -166,7 +174,7 @@
 
     def around(slot, f):
         block = plan[fine_count + slot]
-        return jnp.concatenate([blocks[block, f], blocks[block + 1, f], blocks[block + 2, f]], 0)
+        return jnp.concatenate([blocks[f][block], blocks[f][block + 1], blocks[f][block + 2]], 0)
 
     def ghosts(old, new):
         pairs = [(old[CB - 1:CB], new[CB - 1:CB]), (old[2 * CB:2 * CB + 1], new[2 * CB:2 * CB + 1])]
@@ -311,7 +319,10 @@
     pl.semaphore_wait(barrier, len(greeted))
     for at in range(warm_parts):
         to_core[at].start()
-        to_pair[at].start()
+        if at < AHEAD:
+            to_pair[at].start()
+    for copy in fetched[3:]:
+        copy.wait()
     each_pair(refine_sound)
     for copy in rims:
         copy.start()
@@ -324,13 +335,14 @@
             to_pair[at].wait_recv()
             passed[at].start()
             to_pair[at].wait_send()
-            if at + warm_parts < parts:
-                to_pair[at + warm_parts].start()
+            if at + AHEAD < parts:
+                to_pair[at + AHEAD].start()
         if at >= 1:
             to_core[at - 1].wait_recv()
             passed[at - 1].wait_recv()
             send_along(at - 1)
-            work[at - 1]()
+            for piece in work[(at - 1) * len(work) // parts:at * len(work) // parts]:
+                piece()
 
     for at, (f, r, size) in enumerate(CHUNKS):
         for copy in along[at]:
@@ -360,11 +372,15 @@
             jax.ShapeDtypeStruct(coarse.shape, jnp.float32),
             jax.ShapeDtypeStruct((F_DEV, 3, FB, columns), jnp.float32),
         ),
-        in_specs=[pl.BlockSpec(memory_space=pltpu.SMEM), vmem, vmem, vmem],
+        in_specs=[pl.BlockSpec(memory_space=pltpu.SMEM)] + [pl.BlockSpec(memory_space=pltpu.HBM)] * 4,
         out_specs=(vmem, vmem),
         scratch_shapes=[
+            pltpu.VMEM((1, columns), jnp.float32),
+            pltpu.VMEM(coarse.shape, jnp.float32),
+            *[pltpu.VMEM((B_DEV, CB, columns), jnp.float32)] * 3,
+            pltpu.VMEM(fine.shape, jnp.float32),
+            dma((7,)),
             pltpu.VMEM((2, 3, 3 * RIM, columns), jnp.float32),
-            pltpu.VMEM((B_DEV, 3, CB, columns), jnp.float32),
             pltpu.VMEM((FCAP + 1, 3, CB, columns), jnp.float32),
             pltpu.VMEM((FCAP + 1, 2, 3, RIM, columns), jnp.float32),
             pltpu.VMEM((FCAP, 3, columns // 128, FB, 128), jnp.float32),
@@ -377,12 +393,49 @@
         compiler_params=pltpu.CompilerParams(
             collective_id=0, has_side_effects=True, vmem_limit_bytes=VMEM_LIMIT),
         name="whole_step",
-    )(plan, courant[None, :], coarse, fine)
+    )(plan, courant[None, :], coarse, coarse.reshape(3, B_DEV, CB, columns), fine)
+
+
+def place_kernel(coarse_at, fine_at, coarse_to, fine_to, coarse, fine, in_sems, out_sems):
+    half = coarse.shape[1] // 2
+    views = [(fine_at, fine, fine_to)]
+    for f in range(3):
+        for first in (0, half):
+            views.append([ref.at[f, pl.ds(first, half)] for ref in (coarse_at, coarse, coarse_to)])
+    inward = [pltpu.make_async_copy(source, held, in_sems.at[at])
+              for at, (source, held, target) in enumerate(views)]
+    outward = [pltpu.make_async_copy(held, target, out_sems.at[at])
+               for at, (source, held, target) in enumerate(views)]
+    for copy in inward:
+        copy.start()
+    for come, go in zip(inward, outward):
+        come.wait()
+        go.start()
+    for copy in outward:
+        copy.wait()
+
+
+def place(coarse, fine):
+    hbm = pl.BlockSpec(memory_space=pltpu.HBM)
+    return pl.pallas_call(
+        place_kernel,
+        out_shape=tuple(jax.ShapeDtypeStruct(x.shape, x.dtype) for x in (coarse, fine)),
+        in_specs=[hbm, hbm],
+        out_specs=(hbm, hbm),
+        scratch_shapes=[
+            pltpu.VMEM(coarse.shape, jnp.float32),
+            pltpu.VMEM(fine.shape, jnp.float32),
+            pltpu.SemaphoreType.DMA((7,)),
+            pltpu.SemaphoreType.DMA((7,)),
+        ],
+        compiler_params=pltpu.CompilerParams(vmem_limit_bytes=VMEM_LIMIT),
+        name="place",
+    )(coarse, fine)
 
 
 def per_device(devices, coarse, fine_old, refine_flags, new_slot, courant):
     plan = make_plan(refine_flags, new_slot)
-    return whole_step(devices, plan, courant, coarse, fine_old)
+    return place(*whole_step(devices, plan, courant, coarse, fine_old))
 
 
 def solution(mesh):

time: 39.8 us -> 38.1 us (0.957)
  local copies, waits for them, and re-layouts: 5.62 us -> 0 us
  Pallas kernels: 33.2 us -> 37.3 us
    unnamed x10 -> x0, local copies, waits for them, and re-layouts: 5.62 us -> none
    pallas_call x0 -> x1, Pallas kernels: none -> 2.31 us  [place(): pl.pallas_call(place_kernel, out_shape=tuple((jax.ShapeDtypeStruct(x.shap...]
    pallas_call x1, Pallas kernels: 31.1 us -> 32.8 us  [whole_step(): pl.pallas_call(functools.partial(step_kernel, devices), out_shape=(jax.Sh...]
where the time goes in v4:
time: 38.1 us; the launch traced here: 37.9 us
  Pallas kernels  37.3 us (98%)
  between operations  0.65 us (2%)
    pallas_call x1, Pallas kernels, whole_step(): pl.pallas_call(functools.partial(step_kernel, devices), out_shape=(jax.Sh...  32.8 us
    pallas_call x1, Pallas kernels, place(): pl.pallas_call(place_kernel, out_shape=tuple((jax.ShapeDtypeStruct(x.shap...  2.31 us
    pallas_call x1, Pallas kernels, make_plan(): pl.pallas_call(plan_kernel, out_shape=jax.ShapeDtypeStruct((slots.shape[0...  2.13 us

profile of v4, /device:TPU:0, one launch (start us, length us, event | category | flops | bytes accessed | tf_op | source)
XLA Modules:
  0.0 37.9 jit_solution(9424938903398426540)
XLA Ops:
  0.6 2.1 %make_plan.1.plan = s32[74]{0:T(128)} custom-call(s32[512]{0:T(512)} %flags_at.1, s32[32]{0:T(128)} %slots_at.1), custom_call_target="tpu_custom_call" | custom-call | tf_op jit(solution)/shard_map/make_plan/pallas_call | solution.py:92
  2.8 32.8 %whole_step.1 = (f32[3,512,256]{2,1,0:T(8,128)}, f32[2,3,32,256]{3,2,1,0:T(8,128)}) custom-call(s32[74]{0:T(128)} %make_plan.1.plan, f32[1,256]{1,0:T(1,128)} %bitcast.3, f32[3,512,256]{2,1,0:T(8,128)} %coarse_at.1, f32[3,32,16,256]{3,2,1,0:T(8,128)} %bitcast.2, f32[6,3,32,256]{3,2,1,0:T(8,128)} %fine_at.1), custom_call_target="tpu_custom_call" | custom-call | tf_op jit(solution)/shard_map/whole_step/pallas_call | solution.py:369
  35.6 2.3 %place.1 = (f32[3,512,256]{2,1,0:T(8,128)}, f32[2,3,32,256]{3,2,1,0:T(8,128)}) custom-call(f32[3,512,256]{2,1,0:T(8,128)} %get-tuple-element.4.coarse_at, f32[2,3,32,256]{3,2,1,0:T(8,128)} %get-tuple-element.5.fine_at), custom_call_target="tpu_custom_call" | custom-call | tf_op jit(solution)/shard_map/place/pallas_call | solution.py:420
